TPU v7x, 32 devices: a whole 2x2x4 slice. The times are simulated.
32 devices in a mesh: dp: 4 (over y, x), fsdp: 8 (over z, core).
Axes of the slice: x: 2, y: 2, z: 4, core: 2. Of those that a mesh axis runs over, the one named last changes fastest.
Arguments:
- images: bfloat16 [2048, 16, 256], P(('dp', 'fsdp')), as said below
- partner: int32 [2048], P(('dp', 'fsdp')), may hold values from 0 to 63
- mix_weight: float32 [2048], P(('dp', 'fsdp')), may hold values from 0.2 to 0.8
- labels: int32 [2048], P(('dp', 'fsdp')), may hold values from 0 to 999
- block_master: float32 [3, 1005120], P(None, 'fsdp')
- block_first: float32 [3, 1005120], P(None, 'fsdp')
- block_second: float32 [3, 1005120], P(None, 'fsdp'), as said below
- block_average: float32 [3, 1005120], P(None, 'fsdp')
- head_master: float32 [1610240], P('fsdp')
- head_first: float32 [1610240], P('fsdp')
- head_second: float32 [1610240], P('fsdp'), as said below
- head_average: float32 [1610240], P('fsdp')
- bias_master: float32 [1000], replicated, may hold values from -0.75 to 0.75
- bias_first: float32 [1000], replicated, may hold values from -0.015625 to 0.015625
- bias_second: float32 [1000], replicated, may hold values from 1e-06 to 4e-06
- bias_average: float32 [1000], replicated, may hold values from -0.75 to 0.75
Outputs:
- loss_sum: float32 [], replicated
- block_master_new: float32 [3, 1005120], P(None, 'fsdp')
- block_first_new: float32 [3, 1005120], P(None, 'fsdp')
- block_second_new: float32 [3, 1005120], P(None, 'fsdp')
- block_average_new: float32 [3, 1005120], P(None, 'fsdp')
- head_master_new: float32 [1610240], P('fsdp')
- head_first_new: float32 [1610240], P('fsdp')
- head_second_new: float32 [1610240], P('fsdp')
- head_average_new: float32 [1610240], P('fsdp')
- bias_master_new: float32 [1000], replicated
- bias_first_new: float32 [1000], replicated
- bias_second_new: float32 [1000], replicated
- bias_average_new: float32 [1000], replicated
Inputs may be any that keep to these rules, and one draw needn't show every extreme that they name: The partner of image i is image 64 * floor(i / 64) + partner[i]. `images`: feature maps of order one. `block_second`: positive. `head_second`: positive.
All inputs are finite; a program needn't handle non-finite values.
Results may differ from a plain program's by a relative error of at most 0.028.
Values may be sent and summed in bfloat16 or wider, within the bound.
A program may use at most 320 MiB of HBM per device.

v0:
```python
import jax
import jax.numpy as jnp
from jax import lax
from jax.sharding import PartitionSpec as P

C = 256
E = 1536
SQ = 64
HD = 1280
K = 1000
SIDE = 4
PIX = 16
LAYERS = 3
STEP = 5


EPS_NORM = 0.001
RATE = 0.05
DECAY_WEIGHT = 0.05
BETA_ONE = 0.5
BETA_TWO = 0.5
EPS_ADAM = 1e-08
EMA_RATE = 0.5
SMOOTHING = 0.1
PRECISE = lax.Precision.HIGHEST


def unpack_block(flat):
    lengths = [C * E, E * C, E * SQ, SQ * E, 9 * E, 5 * E, SQ, C, C]
    pieces = []
    offset = 0
    for length_part in lengths:
        pieces.append(lax.slice_in_dim(flat, offset, offset + length_part))
        offset += length_part
    return (
        pieces[0].reshape(C, E),
        pieces[1].reshape(E, C),
        pieces[2].reshape(E, SQ).astype(jnp.float32),
        pieces[3].reshape(SQ, E).astype(jnp.float32),
        pieces[4].reshape(9, E).astype(jnp.float32),
        pieces[5].reshape(5, E).astype(jnp.float32),
        pieces[6].astype(jnp.float32),
        pieces[7].astype(jnp.float32),
        pieces[8].astype(jnp.float32),
    )


def norm_stats(values_in, pixel_total):
    totals = lax.psum(
        (jnp.sum(values_in, axis=(0, 1)), jnp.sum(values_in * values_in, axis=(0, 1))),
        ("dp", "fsdp"),
    )
    mean_val = totals[0] / pixel_total
    return (mean_val, lax.rsqrt(totals[1] / pixel_total - mean_val * mean_val + EPS_NORM))


def norm_back(grad_norm, normed, gain, rstd, pixel_total):
    grad_hat = grad_norm * gain
    totals = lax.psum(
        (jnp.sum(grad_hat, axis=(0, 1)), jnp.sum(grad_hat * normed, axis=(0, 1))), ("dp", "fsdp")
    )
    grad_in = rstd * (grad_hat - totals[0] / pixel_total - normed * (totals[1] / pixel_total))
    return (grad_in, jnp.sum(grad_norm * normed, axis=(0, 1)), jnp.sum(grad_norm, axis=(0, 1)))


def depthwise(field, w_depth):
    images_n = field.shape[0]
    width = field.shape[-1]
    grid = field.reshape(images_n, SIDE, SIDE, width)
    padded = jnp.pad(grid, ((0, 0), (1, 1), (1, 1), (0, 0)))
    result = jnp.zeros_like(grid)
    for tap_row in range(3):
        for tap_col in range(3):
            result = (
                result
                + padded[:, tap_row : tap_row + SIDE, tap_col : tap_col + SIDE, :]
                * w_depth[3 * tap_row + tap_col]
            )
    return result.reshape(images_n, SIDE * SIDE, width)


def spread(pre_one, w_depth):
    return depthwise(jax.nn.silu(pre_one), w_depth)


def excite(pre_two, w_reduce, b_reduce, w_excite, b_excite):
    act_two = jax.nn.silu(pre_two)
    pooled = jnp.mean(act_two, axis=1)
    squeezed = jax.nn.silu(jnp.dot(pooled, w_reduce, precision=PRECISE) + b_reduce)
    gate = jax.nn.sigmoid(jnp.dot(squeezed, w_excite, precision=PRECISE) + b_excite)
    return act_two * gate[:, None, :]


def pool_act(pre_head):
    return jnp.mean(jax.nn.silu(pre_head), axis=1)


def block_forward(stream, gathered, pixel_total):
    w_expand, w_project, w_reduce, w_excite, w_depth, vec_wide, b_reduce, g_proj, b_proj = (
        unpack_block(gathered)
    )
    expanded = jnp.einsum(
        "npc,ce->npe", stream.astype(jnp.bfloat16), w_expand, preferred_element_type=jnp.float32
    )
    stat_one = norm_stats(expanded, pixel_total)
    spread_out = spread((expanded - stat_one[0]) * stat_one[1] * vec_wide[0] + vec_wide[1], w_depth)
    stat_two = norm_stats(spread_out, pixel_total)
    gated = excite(
        (spread_out - stat_two[0]) * stat_two[1] * vec_wide[2] + vec_wide[3],
        w_reduce,
        b_reduce,
        w_excite,
        vec_wide[4],
    )
    projected = jnp.einsum(
        "npe,ec->npc", gated.astype(jnp.bfloat16), w_project, preferred_element_type=jnp.float32
    )
    stat_three = norm_stats(projected, pixel_total)
    return (
        stream + (projected - stat_three[0]) * stat_three[1] * g_proj + b_proj,
        (stat_one, stat_two, stat_three),
    )


def block_backward(stream, grad_out, gathered, layer_stats, pixel_total):
    w_expand, w_project, w_reduce, w_excite, w_depth, vec_wide, b_reduce, g_proj, b_proj = (
        unpack_block(gathered)
    )
    stat_one, stat_two, stat_three = layer_stats
    stream_low = stream.astype(jnp.bfloat16)
    expanded = jnp.einsum("npc,ce->npe", stream_low, w_expand, preferred_element_type=jnp.float32)
    norm_one = (expanded - stat_one[0]) * stat_one[1]
    spread_out, spread_back = jax.vjp(spread, norm_one * vec_wide[0] + vec_wide[1], w_depth)
    norm_two = (spread_out - stat_two[0]) * stat_two[1]
    gated, excite_back = jax.vjp(
        excite, norm_two * vec_wide[2] + vec_wide[3], w_reduce, b_reduce, w_excite, vec_wide[4]
    )
    gated_low = gated.astype(jnp.bfloat16)
    projected = jnp.einsum("npe,ec->npc", gated_low, w_project, preferred_element_type=jnp.float32)
    norm_three = (projected - stat_three[0]) * stat_three[1]
    grad_proj, gain_three, bias_three = norm_back(
        grad_out, norm_three, g_proj, stat_three[1], pixel_total
    )
    grad_proj_low = grad_proj.astype(jnp.bfloat16)
    grad_w_project = jnp.einsum(
        "npe,npc->ec", gated_low, grad_proj_low, preferred_element_type=jnp.float32
    )
    grad_gated = jnp.einsum(
        "npc,ec->npe", grad_proj_low, w_project, preferred_element_type=jnp.float32
    )
    grad_pre_two, grad_w_reduce, grad_b_reduce, grad_w_excite, grad_b_excite = excite_back(
        grad_gated
    )
    grad_spread, gain_two, bias_two = norm_back(
        grad_pre_two, norm_two, vec_wide[2], stat_two[1], pixel_total
    )
    grad_pre_one, grad_w_depth = spread_back(grad_spread)
    grad_expand, gain_one, bias_one = norm_back(
        grad_pre_one, norm_one, vec_wide[0], stat_one[1], pixel_total
    )
    grad_expand_low = grad_expand.astype(jnp.bfloat16)
    grad_w_expand = jnp.einsum(
        "npc,npe->ce", stream_low, grad_expand_low, preferred_element_type=jnp.float32
    )
    grad_stream = grad_out + jnp.einsum(
        "npe,ce->npc", grad_expand_low, w_expand, preferred_element_type=jnp.float32
    )
    flat_grad = jnp.concatenate(
        [
            grad_w_expand.reshape(-1),
            grad_w_project.reshape(-1),
            grad_w_reduce.reshape(-1),
            grad_w_excite.reshape(-1),
            grad_w_depth.reshape(-1),
            jnp.stack([gain_one, bias_one, gain_two, bias_two, grad_b_excite]).reshape(-1),
            grad_b_reduce,
            gain_three,
            bias_three,
        ]
    )
    return (grad_stream, flat_grad)


def adam_update(master, first, second, average, grad):
    first_new = BETA_ONE * first + (1.0 - BETA_ONE) * grad
    second_new = BETA_TWO * second + (1.0 - BETA_TWO) * grad * grad
    fix_one = 1.0 - BETA_ONE**STEP
    fix_two = 1.0 - BETA_TWO**STEP
    master_new = master * (1.0 - RATE * DECAY_WEIGHT) - RATE * (first_new / fix_one) / (
        jnp.sqrt(second_new / fix_two) + EPS_ADAM
    )
    average_new = EMA_RATE * average + (1.0 - EMA_RATE) * master_new
    return (master_new, first_new, second_new, average_new)


def on_device(
    images,
    partner,
    mix_weight,
    labels,
    block_master,
    block_first,
    block_second,
    block_average,
    head_master,
    head_first,
    head_second,
    head_average,
    bias_master,
    bias_first,
    bias_second,
    bias_average,
):
    image_total = images.shape[0] * lax.axis_size("dp") * lax.axis_size("fsdp")
    pixel_total = image_total * PIX
    pictures = images.astype(jnp.float32)
    mix_share = mix_weight[:, None, None]
    stream = mix_share * pictures + (1.0 - mix_share) * jnp.take(pictures, partner, axis=0)
    partner_labels = jnp.take(labels, partner, axis=0)
    inputs_kept = []
    stats_kept = []
    weights_kept = []
    for layer_idx in range(LAYERS):
        gathered = lax.all_gather(
            block_master[layer_idx].astype(jnp.bfloat16), "fsdp", axis=0, tiled=True
        )
        inputs_kept.append(stream)
        weights_kept.append(gathered)
        stream, layer_stats = block_forward(stream, gathered, pixel_total)
        stats_kept.append(layer_stats)
    head_full = lax.all_gather(head_master.astype(jnp.bfloat16), "fsdp", axis=0, tiled=True)
    head_grid = head_full.reshape(HD, C + 2 + K)
    w_conv = head_grid[:, :C]
    gain_head = head_grid[:, C].astype(jnp.float32)
    shift_head = head_grid[:, C + 1].astype(jnp.float32)
    w_class = head_grid[:, C + 2 :]
    stream_low = stream.astype(jnp.bfloat16)
    hidden = jnp.einsum("npc,hc->nph", stream_low, w_conv, preferred_element_type=jnp.float32)
    stat_head = norm_stats(hidden, pixel_total)
    norm_head = (hidden - stat_head[0]) * stat_head[1]
    pooled, pool_back = jax.vjp(pool_act, norm_head * gain_head + shift_head)
    pooled_low = pooled.astype(jnp.bfloat16)
    logits = jnp.dot(pooled_low, w_class, preferred_element_type=jnp.float32) + bias_master
    log_probs = jax.nn.log_softmax(logits, axis=-1)
    classes = jnp.arange(K, dtype=jnp.int32)
    first_hot = (labels[:, None] == classes[None, :]).astype(jnp.float32)
    second_hot = (partner_labels[:, None] == classes[None, :]).astype(jnp.float32)
    weight_col = mix_weight[:, None]
    targets = weight_col * ((1.0 - SMOOTHING) * first_hot + SMOOTHING / K) + (1.0 - weight_col) * (
        (1.0 - SMOOTHING) * second_hot + SMOOTHING / K
    )
    loss_local = -jnp.sum(targets * log_probs)
    grad_logits = (jnp.exp(log_probs) - targets) / image_total
    loss_sum, grad_bias = lax.psum((loss_local, jnp.sum(grad_logits, axis=0)), ("dp", "fsdp"))
    grad_low = grad_logits.astype(jnp.bfloat16)
    grad_w_class = jnp.einsum("nh,nk->hk", pooled_low, grad_low, preferred_element_type=jnp.float32)
    grad_pooled = jnp.einsum("nk,hk->nh", grad_low, w_class, preferred_element_type=jnp.float32)
    grad_pre_head = pool_back(grad_pooled)[0]
    grad_hidden, gain_grad, shift_grad = norm_back(
        grad_pre_head, norm_head, gain_head, stat_head[1], pixel_total
    )
    grad_hidden_low = grad_hidden.astype(jnp.bfloat16)
    grad_w_conv = jnp.einsum(
        "npc,nph->hc", stream_low, grad_hidden_low, preferred_element_type=jnp.float32
    )
    grad_stream = jnp.einsum(
        "nph,hc->npc", grad_hidden_low, w_conv, preferred_element_type=jnp.float32
    )
    head_flat = jnp.concatenate(
        [grad_w_conv, gain_grad[:, None], shift_grad[:, None], grad_w_class], axis=1
    ).reshape(-1)
    head_grad = lax.psum_scatter(
        head_flat.astype(jnp.bfloat16), "fsdp", scatter_dimension=0, tiled=True
    ).astype(jnp.float32)
    grads_list = [None] * LAYERS
    for layer_idx in reversed(range(LAYERS)):
        gathered = lax.all_gather(
            block_master[layer_idx].astype(jnp.bfloat16), "fsdp", axis=0, tiled=True
        )
        grad_stream, flat_grad = block_backward(
            inputs_kept[layer_idx], grad_stream, gathered, stats_kept[layer_idx], pixel_total
        )
        shard_grad = lax.psum_scatter(
            flat_grad.astype(jnp.bfloat16), "fsdp", scatter_dimension=0, tiled=True
        ).astype(jnp.float32)
        grads_list[layer_idx] = shard_grad
    block_grad = jnp.stack(grads_list)
    block_grad, head_grad = (
        lax.psum(block_grad.astype(jnp.bfloat16), "dp").astype(jnp.float32),
        lax.psum(head_grad.astype(jnp.bfloat16), "dp").astype(jnp.float32),
    )
    block_new = adam_update(block_master, block_first, block_second, block_average, block_grad)
    head_new = adam_update(head_master, head_first, head_second, head_average, head_grad)
    bias_new = adam_update(bias_master, bias_first, bias_second, bias_average, grad_bias)
    return (
        loss_sum,
        block_new[0],
        block_new[1],
        block_new[2],
        block_new[3],
        head_new[0],
        head_new[1],
        head_new[2],
        head_new[3],
        bias_new[0],
        bias_new[1],
        bias_new[2],
        bias_new[3],
    )


def solution(mesh):
    in_specs = (
        P(("dp", "fsdp"), None, None),
        P(("dp", "fsdp")),
        P(("dp", "fsdp")),
        P(("dp", "fsdp")),
        P(None, "fsdp"),
        P(None, "fsdp"),
        P(None, "fsdp"),
        P(None, "fsdp"),
        P("fsdp"),
        P("fsdp"),
        P("fsdp"),
        P("fsdp"),
        P(),
        P(),
        P(),
        P(),
    )
    out_specs = (
        P(),
        P(None, "fsdp"),
        P(None, "fsdp"),
        P(None, "fsdp"),
        P(None, "fsdp"),
        P("fsdp"),
        P("fsdp"),
        P("fsdp"),
        P("fsdp"),
        P(),
        P(),
        P(),
        P(),
    )
    return jax.shard_map(
        on_device, mesh=mesh, in_specs=in_specs, out_specs=out_specs, check_vma=False
    )
```

profile of v0, /device:TPU:0, one launch (start us, length us, event | category | flops | bytes accessed | tf_op | source)
XLA Modules:
  0.0 2332.5 jit_solution(3705453531265834363)
XLA Ops:
  43.4 192.4 %all-reduce.94.cloned.1.call-done = (bf16[1610240]{0:T(1024)(128)(2,1)}, bf16[1005120]{0:T(1024)(128)(2,1)}, bf16[1005120]{0:T(1024)(128)(2,1)}, bf16[1005120]{0:T(1024)(128)(2,1)}) async-done(((bf16[1610240]{0:T(1024)(128)(2,1)}, bf16[1005120]{0:T(1024)(128)(2,1)}, bf16[1005120]{0:T(1024)(128)(2,1)}, bf16[1005120]{0:T(1024)(128)(2,1)}), (bf16[1610240]{0:T(1024)(128)(2,1)}, bf16[1005120]{0:T(1024)(128)(2,1)}, ...) | async-done | bytes 9251216
  415.8 40.4 %all-reduce.84 = (f32[1536]{0:T(1024)S(1)}, f32[1536]{0:T(1024)S(1)}) all-reduce(f32[1536]{0:T(1024)S(1)} %get-tuple-element.72, f32[1536]{0:T(1024)S(1)} %get-tuple-element.71), channel_id=1, replica_groups=mesh['dp'=4,'fsdp'=8] {'dp','fsdp'}, use_global_device_ids=true, to_apply=%region_3.4 | all-reduce | flops 3072 | bytes 24576 | tf_op jit(solution)/shard_map/psum | solution.py:49
  469.6 25.2 %fusion.149 = (f32[1536]{0:T(1024)S(1)}, f32[1536]{0:T(1024)S(1)}, f32[64,4,4,1536]{3,2,1,0:T(4,128)}) fusion(f32[1536]{0:T(1024)S(1)} %copy-done.141, f32[1536]{0:T(1024)S(1)} %copy-done.127, f32[1536]{0:T(1024)S(1)} %copy-done.129, f32[1536]{0:T(1024)S(1)} %copy-done.131, f32[64,4,4,1536]{3,2,1,0:T(4,128)} %reshape.593, f32[1536]{0:T(1024)S(1)} %copy-done.133, ...), kind=kLoop, calls=%fused_computation.502 | loop fusion | flops 31454208 | bytes 12650496 | tf_op jit(solution)/shard_map/reduce_sum | solution.py:50
  502.6 39.6 %all-reduce.83 = (f32[1536]{0:T(1024)S(1)}, f32[1536]{0:T(1024)S(1)}) all-reduce(f32[1536]{0:T(1024)S(1)} %get-tuple-element.70, f32[1536]{0:T(1024)S(1)} %get-tuple-element.69), channel_id=1, replica_groups=mesh['dp'=4,'fsdp'=8] {'dp','fsdp'}, use_global_device_ids=true, to_apply=%region_7.8 | all-reduce | flops 3072 | bytes 24576 | tf_op jit(solution)/shard_map/psum | solution.py:49
  563.8 40.8 %all-reduce.82 = (f32[256]{0:T(256)S(1)}, f32[256]{0:T(256)S(1)}) all-reduce(f32[256]{0:T(256)S(1)} %get-tuple-element.110, f32[256]{0:T(256)S(1)} %get-tuple-element.109), channel_id=1, replica_groups=mesh['dp'=4,'fsdp'=8] {'dp','fsdp'}, use_global_device_ids=true, to_apply=%region_12.13 | all-reduce | flops 512 | bytes 4096 | tf_op jit(solution)/shard_map/psum | solution.py:49
  611.4 39.6 %all-reduce.81 = (f32[1536]{0:T(1024)S(1)}, f32[1536]{0:T(1024)S(1)}) all-reduce(f32[1536]{0:T(1024)S(1)} %get-tuple-element.68, f32[1536]{0:T(1024)S(1)} %get-tuple-element.67), channel_id=1, replica_groups=mesh['dp'=4,'fsdp'=8] {'dp','fsdp'}, use_global_device_ids=true, to_apply=%region_16.17 | all-reduce | flops 3072 | bytes 24576 | tf_op jit(solution)/shard_map/psum | solution.py:49
  664.4 25.8 %fusion.147 = (f32[1536]{0:T(1024)S(1)}, f32[1536]{0:T(1024)S(1)}, f32[64,4,4,1536]{3,2,1,0:T(4,128)}) fusion(f32[1536]{0:T(1024)S(1)} %copy-done.159, f32[1536]{0:T(1024)S(1)} %copy-done.145, f32[1536]{0:T(1024)S(1)} %copy-done.147, f32[1536]{0:T(1024)S(1)} %copy-done.149, f32[64,4,4,1536]{3,2,1,0:T(4,128)} %reshape.598, f32[1536]{0:T(1024)S(1)} %copy-done.151, ...), kind=kLoop, calls=%fused_computation.500 | loop fusion | flops 31454208 | bytes 12650496 | tf_op jit(solution)/shard_map/reduce_sum | solution.py:50
  697.8 41.2 %all-reduce.80 = (f32[1536]{0:T(1024)S(1)}, f32[1536]{0:T(1024)S(1)}) all-reduce(f32[1536]{0:T(1024)S(1)} %get-tuple-element.66, f32[1536]{0:T(1024)S(1)} %get-tuple-element.65), channel_id=1, replica_groups=mesh['dp'=4,'fsdp'=8] {'dp','fsdp'}, use_global_device_ids=true, to_apply=%region_20.21 | all-reduce | flops 3072 | bytes 24576 | tf_op jit(solution)/shard_map/psum | solution.py:49
  755.9 39.3 %all-reduce.79 = (f32[256]{0:T(256)S(1)}, f32[256]{0:T(256)S(1)}) all-reduce(f32[256]{0:T(256)S(1)} %get-tuple-element.108, f32[256]{0:T(256)S(1)} %get-tuple-element.107), channel_id=1, replica_groups=mesh['dp'=4,'fsdp'=8] {'dp','fsdp'}, use_global_device_ids=true, to_apply=%region_25.26 | all-reduce | flops 512 | bytes 4096 | tf_op jit(solution)/shard_map/psum | solution.py:49
  801.3 41.4 %all-reduce.78 = (f32[1536]{0:T(1024)S(1)}, f32[1536]{0:T(1024)S(1)}) all-reduce(f32[1536]{0:T(1024)S(1)} %get-tuple-element.64, f32[1536]{0:T(1024)S(1)} %get-tuple-element.63), channel_id=1, replica_groups=mesh['dp'=4,'fsdp'=8] {'dp','fsdp'}, use_global_device_ids=true, to_apply=%region_29.30 | all-reduce | flops 3072 | bytes 24576 | tf_op jit(solution)/shard_map/psum | solution.py:49
  856.1 25.5 %fusion.145 = (f32[1536]{0:T(1024)S(1)}, f32[1536]{0:T(1024)S(1)}, f32[64,4,4,1536]{3,2,1,0:T(4,128)}) fusion(f32[1536]{0:T(1024)S(1)} %copy-done.177, f32[1536]{0:T(1024)S(1)} %copy-done.163, f32[1536]{0:T(1024)S(1)} %copy-done.165, f32[1536]{0:T(1024)S(1)} %copy-done.167, f32[64,4,4,1536]{3,2,1,0:T(4,128)} %reshape.603, f32[1536]{0:T(1024)S(1)} %copy-done.169, ...), kind=kLoop, calls=%fused_computation.498 | loop fusion | flops 31454208 | bytes 12650496 | tf_op jit(solution)/shard_map/reduce_sum | solution.py:50
  889.3 39.6 %all-reduce.77 = (f32[1536]{0:T(1024)S(1)}, f32[1536]{0:T(1024)S(1)}) all-reduce(f32[1536]{0:T(1024)S(1)} %get-tuple-element.62, f32[1536]{0:T(1024)S(1)} %get-tuple-element.61), channel_id=1, replica_groups=mesh['dp'=4,'fsdp'=8] {'dp','fsdp'}, use_global_device_ids=true, to_apply=%region_33.34 | all-reduce | flops 3072 | bytes 24576 | tf_op jit(solution)/shard_map/psum | solution.py:49
  944.6 41.0 %all-reduce.76 = (f32[256]{0:T(256)S(1)}, f32[256]{0:T(256)S(1)}) all-reduce(f32[256]{0:T(256)S(1)} %get-tuple-element.106, f32[256]{0:T(256)S(1)} %get-tuple-element.105), channel_id=1, replica_groups=mesh['dp'=4,'fsdp'=8] {'dp','fsdp'}, use_global_device_ids=true, to_apply=%region_38.39 | all-reduce | flops 512 | bytes 4096 | tf_op jit(solution)/shard_map/psum | solution.py:49
  990.9 39.5 %all-reduce.75 = (f32[1280]{0:T(1024)S(1)}, f32[1280]{0:T(1024)S(1)}) all-reduce(f32[1280]{0:T(1024)S(1)} %get-tuple-element.78, f32[1280]{0:T(1024)S(1)} %get-tuple-element.77), channel_id=1, replica_groups=mesh['dp'=4,'fsdp'=8] {'dp','fsdp'}, use_global_device_ids=true, to_apply=%region_42.43 | all-reduce | flops 2560 | bytes 20480 | tf_op jit(solution)/shard_map/psum | solution.py:49
  1045.0 41.4 %all-reduce.74 = (f32[1280]{0:T(1024)S(1)}, f32[1280]{0:T(1024)S(1)}) all-reduce(f32[1280]{0:T(1024)S(1)} %get-tuple-element.75, f32[1280]{0:T(1024)S(1)} %get-tuple-element.76), channel_id=1, replica_groups=mesh['dp'=4,'fsdp'=8] {'dp','fsdp'}, use_global_device_ids=true, to_apply=%region_51.52 | all-reduce | flops 2560 | bytes 20480 | tf_op jit(solution)/shard_map/psum | solution.py:59
  1099.5 39.6 %all-reduce.73 = (f32[256]{0:T(256)S(1)}, f32[256]{0:T(256)S(1)}) all-reduce(f32[256]{0:T(256)S(1)} %get-tuple-element.98, f32[256]{0:T(256)S(1)} %get-tuple-element.99), channel_id=1, replica_groups=mesh['dp'=4,'fsdp'=8] {'dp','fsdp'}, use_global_device_ids=true, to_apply=%region_55.56 | all-reduce | flops 512 | bytes 4096 | tf_op jit(solution)/shard_map/psum | solution.py:59
  1162.3 41.3 %all-reduce.72 = (f32[1536]{0:T(1024)S(1)}, f32[1536]{0:T(1024)S(1)}) all-reduce(f32[1536]{0:T(1024)S(1)} %get-tuple-element.22, f32[1536]{0:T(1024)S(1)} %get-tuple-element.50), channel_id=1, replica_groups=mesh['dp'=4,'fsdp'=8] {'dp','fsdp'}, use_global_device_ids=true, to_apply=%region_60.61 | all-reduce | flops 3072 | bytes 24576 | tf_op jit(solution)/shard_map/psum | solution.py:59
  1222.2 37.3 %multiply_reduce_fusion.10 = (f32[1536]{0:T(1024)}, f32[1536]{0:T(1024)}, f32[1536]{0:T(1024)}, f32[1536]{0:T(1024)}, f32[1536]{0:T(1024)}, /*index=5*/f32[1536]...) fusion(f32[64,4,4,1536]{3,2,1,0:T(4,128)} %reshape.609, ...), kind=kLoop, calls=%fused_computation.79 | loop fusion | flops 39309312 | bytes 69310464 | tf_op jit(solution)/shard_map/transpose(jvp())/reduce_sum | solution.py:76
  1311.5 39.2 %all-reduce.71 = (f32[1536]{0:T(1024)S(1)}, f32[1536]{0:T(1024)S(1)}) all-reduce(f32[1536]{0:T(1024)S(1)} %get-tuple-element.24, f32[1536]{0:T(1024)S(1)} %get-tuple-element.49), channel_id=1, replica_groups=mesh['dp'=4,'fsdp'=8] {'dp','fsdp'}, use_global_device_ids=true, to_apply=%region_64.65 | all-reduce | flops 3072 | bytes 24576 | tf_op jit(solution)/shard_map/psum | solution.py:59
  1361.9 41.3 %all-reduce.70 = (f32[256]{0:T(256)}, f32[256]{0:T(256)}) all-reduce(f32[256]{0:T(256)} %get-tuple-element.96, f32[256]{0:T(256)} %get-tuple-element.100), channel_id=1, replica_groups=mesh['dp'=4,'fsdp'=8] {'dp','fsdp'}, use_global_device_ids=true, to_apply=%region_68.69 | all-reduce | flops 512 | bytes 4096 | tf_op jit(solution)/shard_map/psum | solution.py:59
  1427.6 39.7 %all-reduce.69 = (f32[1536]{0:T(1024)S(1)}, f32[1536]{0:T(1024)S(1)}) all-reduce(f32[1536]{0:T(1024)S(1)} %get-tuple-element.18, f32[1536]{0:T(1024)S(1)} %get-tuple-element.52), channel_id=1, replica_groups=mesh['dp'=4,'fsdp'=8] {'dp','fsdp'}, use_global_device_ids=true, to_apply=%region_73.74 | all-reduce | flops 3072 | bytes 24576 | tf_op jit(solution)/shard_map/psum | solution.py:59
  1485.9 37.2 %multiply_reduce_fusion.21 = (f32[1536]{0:T(1024)}, f32[1536]{0:T(1024)}, f32[1536]{0:T(1024)}, f32[1536]{0:T(1024)}, f32[1536]{0:T(1024)}, /*index=5*/f32[1536]...) fusion(f32[64,4,4,1536]{3,2,1,0:T(4,128)} %reshape.612, ...), kind=kLoop, calls=%fused_computation.91 | loop fusion | flops 39309312 | bytes 69310464 | tf_op jit(solution)/shard_map/transpose(jvp())/reduce_sum | solution.py:76
  1574.8 41.1 %all-reduce.68 = (f32[1536]{0:T(1024)S(1)}, f32[1536]{0:T(1024)S(1)}) all-reduce(f32[1536]{0:T(1024)S(1)} %get-tuple-element.20, f32[1536]{0:T(1024)S(1)} %get-tuple-element.51), channel_id=1, replica_groups=mesh['dp'=4,'fsdp'=8] {'dp','fsdp'}, use_global_device_ids=true, to_apply=%region_77.78 | all-reduce | flops 3072 | bytes 24576 | tf_op jit(solution)/shard_map/psum | solution.py:59
  1627.2 39.4 %all-reduce.67 = (f32[256]{0:T(256)S(1)}, f32[256]{0:T(256)S(1)}) all-reduce(f32[256]{0:T(256)S(1)} %get-tuple-element.94, f32[256]{0:T(256)S(1)} %get-tuple-element.101), channel_id=1, replica_groups=mesh['dp'=4,'fsdp'=8] {'dp','fsdp'}, use_global_device_ids=true, to_apply=%region_81.82 | all-reduce | flops 512 | bytes 4096 | tf_op jit(solution)/shard_map/psum | solution.py:59
  1757.8 41.4 %all-reduce.66 = (f32[1536]{0:T(1024)S(1)}, f32[1536]{0:T(1024)S(1)}) all-reduce(f32[1536]{0:T(1024)S(1)} %get-tuple-element.14, f32[1536]{0:T(1024)S(1)} %get-tuple-element.54), channel_id=1, replica_groups=mesh['dp'=4,'fsdp'=8] {'dp','fsdp'}, use_global_device_ids=true, to_apply=%region_86.87 | all-reduce | flops 3072 | bytes 24576 | tf_op jit(solution)/shard_map/psum | solution.py:59
  1818.3 39.8 %multiply_reduce_fusion.32 = (f32[1536]{0:T(1024)S(1)}, f32[1536]{0:T(1024)S(1)}, f32[1536]{0:T(1024)S(1)}, f32[1536]{0:T(1024)S(1)}, f32[1536]{0:T(1024)S(1)}, ...) fusion(f32[64,4,4,1536]{3,2,1,0:T(4,128)} %reshape.615, ...), kind=kLoop, calls=%fused_computation.103 | loop fusion | flops 39309312 | bytes 69310464 | tf_op jit(solution)/shard_map/transpose(jvp())/reduce_sum | solution.py:76
  1912.8 39.6 %all-reduce.65 = (f32[]{:T(128)}, f32[1536]{0:T(1024)S(1)}, f32[1536]{0:T(1024)S(1)}, f32[1000]{0:T(1024)}) all-reduce(f32[]{:T(128)S(6)} %neg.84, f32[1536]{0:T(1024)S(1)} %get-tuple-element.16, f32[1536]{0:T(1024)S(1)} %get-tuple-element.53, f32[1000]{0:T(1024)S(1)} %copy-done.196), channel_id=1, replica_groups=mesh['dp'=4,'fsdp'=8] {'dp','fsdp'}, use_global_device_ids=true, to_apply=%region_47.48 | all-reduce | flops 4073 | bytes 32584 | tf_op jit(solution)/shard_map/psum | solution.py:254
  1962.5 31.1 %concatenate.18 = bf16[1005120]{0:T(1024)(128)(2,1)} concatenate(bf16[393216]{0:T(1024)(128)(2,1)} %reshape.631, bf16[393216]{0:T(1024)(128)(2,1)S(1)} %bitcast.129, bf16[98304]{0:T(1024)(128)(2,1)} %reshape.633, bf16[98304]{0:T(1024)(128)(2,1)S(1)} %reshape.634, bf16[13824]{0:T(1024)(128)(2,1)} %reshape.635, bf16[7680]{0:T(1024)(128)(2,1)} %reshape.637, ...), dimensions={0} | concatenate | bytes 4020480 | tf_op jit(solution)/shard_map/concatenate | solution.py:168
  1993.6 31.2 %concatenate.17 = bf16[1005120]{0:T(1024)(128)(2,1)} concatenate(bf16[393216]{0:T(1024)(128)(2,1)} %reshape.624, bf16[393216]{0:T(1024)(128)(2,1)S(1)} %bitcast.130, bf16[98304]{0:T(1024)(128)(2,1)} %reshape.626, bf16[98304]{0:T(1024)(128)(2,1)S(1)} %reshape.627, bf16[13824]{0:T(1024)(128)(2,1)} %reshape.628, bf16[7680]{0:T(1024)(128)(2,1)} %reshape.630, ...), dimensions={0} | concatenate | bytes 4020480 | tf_op jit(solution)/shard_map/concatenate | solution.py:168
  2024.8 27.8 %concatenate.16 = bf16[1005120]{0:T(1024)(128)(2,1)} concatenate(bf16[393216]{0:T(1024)(128)(2,1)S(1)} %reshape.617, bf16[393216]{0:T(1024)(128)(2,1)S(1)} %bitcast.131, bf16[98304]{0:T(1024)(128)(2,1)} %reshape.619, bf16[98304]{0:T(1024)(128)(2,1)} %reshape.620, bf16[13824]{0:T(1024)(128)(2,1)} %reshape.621, bf16[7680]{0:T(1024)(128)(2,1)S(1)} %copy-done.179, ...), dimensions={0} | concatenate | bytes 4020480 | tf_op jit(solution)/shard_map/concatenate | solution.py:168
  2054.3 192.7 %all-reduce.92.cloned.1.call-done = (bf16[1005120]{0:T(1024)(128)(2,1)}, bf16[1005120]{0:T(1024)(128)(2,1)}, bf16[1005120]{0:T(1024)(128)(2,1)}, bf16[1610240]{0:T(1024)(128)(2,1)}) async-done(((bf16[1005120]{0:T(1024)(128)(2,1)}, bf16[1005120]{0:T(1024)(128)(2,1)}, bf16[1005120]{0:T(1024)(128)(2,1)}, bf16[1610240]{0:T(1024)(128)(2,1)}), (bf16[1005120]{0:T(1024)(128)(2,1)}, bf16[1005120]{0:T(1024)(128)(2,1)}, ...) | async-done | bytes 9251216
  2256.9 57.8 %all-reduce.96.cloned.1.call-done = (bf16[3,125640]{1,0:T(4,128)(2,1)}, bf16[201280]{0:T(1024)(128)(2,1)}) async-done(((bf16[3,125640]{1,0:T(4,128)(2,1)}, bf16[201280]{0:T(1024)(128)(2,1)}), (bf16[3,125640]{1,0:T(4,128)(2,1)}, bf16[201280]{0:T(1024)(128)(2,1)})) %all-reduce.96.cloned.1.call-update) | async-done | bytes 1156416 | tf_op jit(solution)/shard_map/psum | solution.py:289
  (753 shorter events, 781.8 us)
Async XLA Ops:
  7.2 228.7 %all-reduce.94.cloned.1.call-start = ((), (), s32[]{:S(2)}) async-start(), calls=%async_computation.1 | async-start | bytes 18509824
  39.3 2207.7 %all-reduce.92.cloned.1.call-start = ((), (), s32[]{:S(2)}) async-start(), calls=%async_computation | async-start | bytes 18509824
  42.2 562.4 %copy-start.3 = (f32[64,16,256]{2,1,0:T(8,128)}, f32[64,16,256]{2,1,0:T(8,128)S(1)}, u32[]{:S(2)}) copy-start(f32[64,16,256]{2,1,0:T(8,128)S(1)} %gather_fusion.1) | copy-start | bytes 3145732
  386.4 162.9 %copy-start.34 = (bf16[1536,64]{1,0:T(8,128)(2,1)}, bf16[1536,64]{1,0:T(8,128)(2,1)S(1)}, u32[]{:S(2)}) copy-start(bf16[1536,64]{1,0:T(8,128)(2,1)S(1)} %reshape.594) | copy-start | bytes 589828
  391.6 259.4 %copy-start.73 = (f32[1536]{0:T(1024)}, f32[1536]{0:T(1024)S(1)}, u32[]{:S(2)}) copy-start(f32[1536]{0:T(1024)S(1)} %get-tuple-element.152) | copy-start | bytes 18436
  391.6 259.4 %copy-start.91 = (f32[1536]{0:T(1024)}, f32[1536]{0:T(1024)S(1)}, u32[]{:S(2)}) copy-start(f32[1536]{0:T(1024)S(1)} %get-tuple-element.151) | copy-start | bytes 18436
  391.6 347.4 %copy-start.98 = (f32[1536]{0:T(1024)}, f32[1536]{0:T(1024)S(1)}, u32[]{:S(2)}) copy-start(f32[1536]{0:T(1024)S(1)} %get-tuple-element.150) | copy-start | bytes 18436
  391.6 347.4 %copy-start.121 = (f32[1536]{0:T(1024)}, f32[1536]{0:T(1024)S(1)}, u32[]{:S(2)}) copy-start(f32[1536]{0:T(1024)S(1)} %get-tuple-element.149) | copy-start | bytes 18436
  393.3 271.0 %copy-start.143 = (f32[1536]{0:T(1024)}, f32[1536]{0:T(1024)S(1)}, u32[]{:S(2)}) copy-start(f32[1536]{0:T(1024)S(1)} %get-tuple-element.125) | copy-start | bytes 18436
  395.5 350.6 %copy-start.36 = (bf16[1536,64]{1,0:T(8,128)(2,1)}, bf16[1536,64]{1,0:T(8,128)(2,1)S(1)}, u32[]{:S(2)}) copy-start(bf16[1536,64]{1,0:T(8,128)(2,1)S(1)} %reshape.599) | copy-start | bytes 589828
  403.3 53.0 %copy-start.83 = (f32[1536]{0:T(1024)S(1)}, f32[1536]{0:T(1024)}, u32[]{:S(2)}) copy-start(f32[1536]{0:T(1024)} %get-tuple-element.157) | copy-start | bytes 18436
  403.3 53.0 %copy-start.89 = (f32[1536]{0:T(1024)S(1)}, f32[1536]{0:T(1024)}, u32[]{:S(2)}) copy-start(f32[1536]{0:T(1024)} %get-tuple-element.156) | copy-start | bytes 18436
  406.6 529.5 %copy-start.38 = (bf16[1536,64]{1,0:T(8,128)(2,1)}, bf16[1536,64]{1,0:T(8,128)(2,1)S(1)}, u32[]{:S(2)}) copy-start(bf16[1536,64]{1,0:T(8,128)(2,1)S(1)} %reshape.604) | copy-start | bytes 589828
  563.8 92.7 %copy-start.24 = (f32[64,16,256]{2,1,0:T(8,128)}, f32[64,16,256]{2,1,0:T(8,128)S(1)}, u32[]{:S(2)}) copy-start(f32[64,16,256]{2,1,0:T(8,128)S(1)} %get-tuple-element.301) | copy-start | bytes 3145732
  755.8 92.4 %copy-start.26 = (f32[64,16,256]{2,1,0:T(8,128)}, f32[64,16,256]{2,1,0:T(8,128)S(1)}, u32[]{:S(2)}) copy-start(f32[64,16,256]{2,1,0:T(8,128)S(1)} %get-tuple-element.303) | copy-start | bytes 3145732
  755.9 86.8 %copy-start.93 = (f32[1536]{0:T(1024)S(1)}, f32[1536]{0:T(1024)}, u32[]{:S(2)}) copy-start(f32[1536]{0:T(1024)} %get-tuple-element.146) | copy-start | bytes 18436
  941.4 89.0 %copy-start.116 = (f32[1280]{0:T(1024)S(1)}, f32[1280]{0:T(1024)}, u32[]{:S(2)}) copy-start(f32[1280]{0:T(1024)} %get-tuple-element.91) | copy-start | bytes 15364
  941.4 89.0 %copy-start.117 = (f32[1280]{0:T(1024)S(1)}, f32[1280]{0:T(1024)}, u32[]{:S(2)}) copy-start(f32[1280]{0:T(1024)} %get-tuple-element.92) | copy-start | bytes 15364
  1746.2 53.0 %copy-start.84 = (f32[1536]{0:T(1024)S(1)}, f32[1536]{0:T(1024)}, u32[]{:S(2)}) copy-start(f32[1536]{0:T(1024)} %get-tuple-element.157) | copy-start | bytes 18436
  1746.2 53.0 %copy-start.86 = (f32[1536]{0:T(1024)S(1)}, f32[1536]{0:T(1024)}, u32[]{:S(2)}) copy-start(f32[1536]{0:T(1024)} %copy-done.85) | copy-start | bytes 18436
  1746.2 53.0 %copy-start.88 = (f32[1536]{0:T(1024)S(1)}, f32[1536]{0:T(1024)}, u32[]{:S(2)}) copy-start(f32[1536]{0:T(1024)} %copy-done.87) | copy-start | bytes 18436
  1746.2 53.0 %copy-start.90 = (f32[1536]{0:T(1024)S(1)}, f32[1536]{0:T(1024)}, u32[]{:S(2)}) copy-start(f32[1536]{0:T(1024)} %get-tuple-element.156) | copy-start | bytes 18436
  1960.4 64.4 %copy-start.42 = (bf16[192,2,8,128]{3,1,2,0:T(2,128)(2,1)S(1)}, bf16[192,2,8,128]{3,1,2,0:T(2,128)(2,1)}, u32[]{:S(2)}) copy-start(bf16[192,2,8,128]{3,1,2,0:T(2,128)(2,1)} %copy.65) | copy-start | bytes 2359300
  1960.4 64.4 %copy-start.179 = (bf16[7680]{0:T(1024)(128)(2,1)S(1)}, bf16[7680]{0:T(1024)(128)(2,1)}, u32[]{:S(2)}) copy-start(bf16[7680]{0:T(1024)(128)(2,1)} %reshape.623) | copy-start | bytes 46084
  2052.6 203.6 %copy-start.219 = (f32[1000]{0:T(1024)S(1)}, f32[1000]{0:T(1024)}, u32[]{:S(2)}) copy-start(f32[1000]{0:T(1024)} %param.28) | copy-start | bytes 12004
  2052.6 203.6 %copy-start.220 = (f32[1000]{0:T(1024)S(1)}, f32[1000]{0:T(1024)}, u32[]{:S(2)}) copy-start(f32[1000]{0:T(1024)} %param.31) | copy-start | bytes 12004
  2052.6 203.6 %copy-start.221 = (f32[1000]{0:T(1024)S(1)}, f32[1000]{0:T(1024)}, u32[]{:S(2)}) copy-start(f32[1000]{0:T(1024)} %param.29) | copy-start | bytes 12004
  2052.7 203.6 %copy-start.222 = (f32[1000]{0:T(1024)S(1)}, f32[1000]{0:T(1024)}, u32[]{:S(2)}) copy-start(f32[1000]{0:T(1024)} %param.30) | copy-start | bytes 12004
  2052.7 203.6 %copy-start.223 = (f32[1000]{0:T(1024)S(1)}, f32[1000]{0:T(1024)}, u32[]{:S(2)}) copy-start(f32[1000]{0:T(1024)} %get-tuple-element.161) | copy-start | bytes 12004
  2052.7 262.0 %copy-start.40 = (f32[201280]{0:T(1024)S(1)}, f32[201280]{0:T(1024)}, u32[]{:S(2)}) copy-start(f32[201280]{0:T(1024)} %param.24) | copy-start | bytes 2415364
  2052.7 262.0 %all-reduce.96.cloned.1.call-start = ((), (), s32[]{:S(2)}) async-start(), calls=%async_computation.2 | async-start | bytes 2818048 | tf_op jit(solution)/shard_map/psum | solution.py:289
  2251.0 67.7 %copy-start.22 = (f32[3,125640]{1,0:T(4,128)S(1)}, f32[3,125640]{1,0:T(4,128)}, u32[]{:S(2)}) copy-start(f32[3,125640]{1,0:T(4,128)} %param.20) | copy-start | bytes 4523044
  (207 other events, 3370.1 us)
Sparse Core Ops, SparseCore 0:
  39.5 196.3 all-reduce.93
  2052.7 194.2 all-reduce.91
  2256.3 58.2 all-reduce.95
where the time goes:
time: 2350 us; the launch traced here: 2330 us
  blocking collectives  806 us (34%)
  other arithmetic  492 us (21%)
  local copies, waits for them, and re-layouts  468 us (20%)
  waiting for transfers between devices  443 us (19%)
  matrix products  102 us (4%)
    psum x10, blocking collectives, norm_stats(): lax.psum((jnp.sum(values_in, axis=(0, 1)), jnp.sum(values_in * values_in,...  402 us
    unnamed x5, waiting for transfers between devices  385 us
    psum x9, blocking collectives, norm_back(): lax.psum((jnp.sum(grad_hat, axis=(0, 1)), jnp.sum(grad_hat * normed, axis...  364 us
    reduce_sum x6, other arithmetic, depthwise(): padded[:, tap_row:tap_row + SIDE, tap_col:tap_col + SIDE, :]  146 us
    unnamed x491, local copies, waits for them, and re-layouts  110 us
    add_any x6, other arithmetic, depthwise(): padded[:, tap_row:tap_row + SIDE, tap_col:tap_col + SIDE, :]  105 us
    concatenate x3, local copies, waits for them, and re-layouts, block_backward(): jnp.concatenate([grad_w_expand.reshape(-1), grad_w_project.reshape(-1), g...  90.1 us
    reduce_sum x3, other arithmetic, norm_stats(): jnp.sum(values_in, axis=(0, 1))  76.5 us
  transfers between devices with their start and end apart: 3, of which 3 were waited for; matrix products, arithmetic and copies ran while one was open for 0% of the time, Pallas kernels for 0%

commit v1 on v0

v1 whole, which is shorter than its diff:
```python
import functools

import jax
import jax.numpy as jnp
from jax import lax
from jax.experimental import pallas as pl
from jax.experimental.pallas import tpu as pltpu
from jax.sharding import PartitionSpec as P

C = 256
E = 1536
SQ = 64
K = 1000
SIDE = 4
PIX = 16
LAYERS = 3
STEP = 5
EPS_NORM = 0.001
RATE = 0.05
DECAY_WEIGHT = 0.05
BETA_ONE = 0.5
BETA_TWO = 0.5
EPS_ADAM = 1e-08
EMA_RATE = 0.5
SMOOTHING = 0.1

LANE = 128
KP = 1024
HEAD_W = C + LANE + KP
PB = 2 * C * E + 2 * E * SQ + 14 * E + SQ + 2 * C
ROW_P = C * E // LANE
ROW_R = ROW_P + E * C // LANE
ROW_X = ROW_R + E * SQ // LANE
ROW_D = ROW_X + SQ * E // LANE
ROW_S = ROW_D + 14 * E // LANE
NJ = E // LANE
GROUPS = 2
GW = E // GROUPS
MBLK = 4

MESH = pl.DeviceIdType.MESH
F32 = jnp.float32
BF16 = jnp.bfloat16
HIGH = lax.Precision.HIGHEST
VMEM_LIMIT = 60 * 1024 * 1024
VM = pl.BlockSpec(memory_space=pltpu.VMEM)


def ceil_to(value, unit):
    return -(-value // unit) * unit


class Plan:
    def __init__(self, mesh, images, head_rows):
        self.nd = mesh.shape["dp"]
        self.nf = mesh.shape["fsdp"]
        self.devices = self.nd * self.nf
        self.images = images
        self.rows = images * PIX
        self.count = float(self.rows * self.devices)
        self.shard = PB // self.nf
        self.base = [(self.shard * f // LANE) // 16 * 16 for f in range(self.nf)]
        self.chunk = ceil_to(-(-self.shard // LANE) + 17, 16)
        self.flat = self.base[-1] + self.chunk
        self.head_pad = ceil_to(head_rows, 16)
        self.hd = self.head_pad * self.nf
        self.head_rows = head_rows


def dot(a, b, dims=((1,), (0,)), precision=None):
    return lax.dot_general(a, b, (dims, ((), ())), precision=precision, preferred_element_type=F32)


def row_sum(value):
    return jnp.sum(value, axis=0, keepdims=True)


def my_index(plan):
    return lax.axis_index("dp") * plan.nf + lax.axis_index("fsdp")


def peer_id(plan, step):
    k = lax.rem(my_index(plan) + step, plan.devices)
    return (k // plan.nf, lax.rem(k, plan.nf))


def enter(plan):
    barrier = pltpu.get_barrier_semaphore()

    def greet(step, carry):
        pl.semaphore_signal(barrier, inc=1, device_id=peer_id(plan, step), device_id_type=MESH)
        return carry

    lax.fori_loop(1, plan.devices, greet, 0)


def entered(plan):
    pl.semaphore_wait(pltpu.get_barrier_semaphore(), plan.devices - 1)


def share(plan, buf, send, recv, first, second):
    buf[0, 0:1, :] = first
    buf[0, 1:2, :] = second

    def push(step, carry):
        pltpu.make_async_remote_copy(
            src_ref=buf.at[0],
            dst_ref=buf.at[step],
            send_sem=send,
            recv_sem=recv,
            device_id=peer_id(plan, step),
            device_id_type=MESH,
        ).start()
        return carry

    lax.fori_loop(1, plan.devices, push, 0)


def collect(plan, buf, send, recv):
    others = buf.at[pl.ds(1, plan.devices - 1)]
    pltpu.make_async_copy(others, others, recv).wait()
    total = jnp.sum(buf[...], axis=0)
    return total[0:1, :], total[1:2, :]


def finish(plan, buf, send, recv):
    others = buf.at[pl.ds(1, plan.devices - 1)]
    pltpu.make_async_copy(others, others, send).wait()


def exchange_scratch(plan, widths):
    shapes = [pltpu.VMEM((plan.devices, 2, w), F32) for w in widths]
    sems = [pltpu.SemaphoreType.DMA(()) for w in widths]
    return shapes + sems + sems


def exchange_refs(refs, n):
    return [(refs[i], refs[n + i], refs[2 * n + i]) for i in range(n)]


def moments(plan, pair):
    mean = pair[0] / plan.count
    return mean, lax.rsqrt(pair[1] / plan.count - mean * mean + EPS_NORM)


def taps():
    found = []
    for y in range(SIDE):
        for x in range(SIDE):
            for a in range(3):
                for b in range(3):
                    iy, ix = y + a - 1, x + b - 1
                    if 0 <= iy < SIDE and 0 <= ix < SIDE:
                        found.append((y * SIDE + x, 3 * a + b, iy * SIDE + ix))
    return found


TAPS = taps()


def half_tanh(half):
    return jnp.tanh(half)


def silu(z):
    half = 0.5 * z
    return half * half_tanh(half) + half


def sigmoid(z):
    return 0.5 * half_tanh(0.5 * z) + 0.5


def silu_slope(z):
    half = 0.5 * z
    t = half_tanh(half)
    return 0.5 * (1.0 + t + half * (1.0 - t * t))


def lanes(j):
    return pl.ds(pl.multiple_of(j * LANE, LANE), LANE)


def images_at(b):
    return pl.ds(pl.multiple_of(b * 8, 8), 8)


def over_tiles(plan, first_chunk, chunks, per_chunk, body, n_sums, store_sums):
    def chunk_step(jj, carry):
        j = first_chunk + jj
        hoisted = per_chunk(j)
        zero = tuple(jnp.zeros((8, LANE), F32) for _ in range(n_sums))
        sums = lax.fori_loop(
            0, plan.images // 8, lambda b, s: body(j, b, hoisted, s), zero
        )
        store_sums(j, sums)
        return carry

    lax.fori_loop(0, chunks, chunk_step, 0)


def unpack_kernel(plan, got, we, wp, wr, wx, small, tail, flat):
    lane = lax.broadcasted_iota(jnp.int32, (1, LANE), 1)
    low = lane < SQ
    for f in range(plan.nf):
        base, at = plan.base[f], f * plan.chunk
        head = got[at : at + 16, :].astype(F32)
        if f:
            head = head + flat[base : base + 16, :]
        flat[base : base + 16, :] = head
        flat[base + 16 : base + plan.chunk, :] = got[at + 16 : at + plan.chunk, :].astype(F32)
    for j in range(NJ):
        cols = slice(j * LANE, (j + 1) * LANE)
        we[:, cols] = flat[pl.ds(j, C, stride=NJ), :].astype(BF16)
        wx[0:SQ, cols] = flat[pl.ds(ROW_X + j, SQ, stride=NJ), :]
        wx[SQ:LANE, cols] = jnp.zeros((LANE - SQ, LANE), F32)
        small[0:14, cols] = flat[pl.ds(ROW_D + j, 14, stride=NJ), :]
        small[14:16, cols] = jnp.zeros((2, LANE), F32)
    for h in range(C // LANE):
        wp[:, h * LANE : (h + 1) * LANE] = flat[pl.ds(ROW_P + h, E, stride=2), :].astype(BF16)
    pairs = flat[ROW_R:ROW_X, :]
    wr[pl.ds(0, E // 2, stride=2), :] = jnp.where(low, pairs, 0.0)
    wr[pl.ds(1, E // 2, stride=2), :] = jnp.where(low, pltpu.roll(pairs, SQ, 1), 0.0)
    rows = [flat[ROW_S + i : ROW_S + i + 1, :] for i in range(5)]
    turned = [pltpu.roll(jnp.broadcast_to(r, (8, LANE)), SQ, 1)[0:1, :] for r in rows]
    tail[...] = jnp.zeros((8, C), F32)
    tail[0:1, 0:LANE] = jnp.where(low, rows[0], 0.0)
    for i, at in ((1, 0), (2, 2)):
        tail[i : i + 1, 0:LANE] = jnp.where(low, turned[at], turned[at + 1])
        tail[i : i + 1, LANE:C] = jnp.where(low, turned[at + 1], turned[at + 2])


def unpack(plan, gathered):
    return pl.pallas_call(
        functools.partial(unpack_kernel, plan),
        out_shape=(
            jax.ShapeDtypeStruct((C, E), BF16),
            jax.ShapeDtypeStruct((E, C), BF16),
            jax.ShapeDtypeStruct((E, LANE), F32),
            jax.ShapeDtypeStruct((LANE, E), F32),
            jax.ShapeDtypeStruct((16, E), F32),
            jax.ShapeDtypeStruct((8, C), F32),
        ),
        in_specs=[VM],
        out_specs=(VM,) * 6,
        scratch_shapes=[pltpu.VMEM((plan.flat, LANE), F32)],
        compiler_params=pltpu.CompilerParams(vmem_limit_bytes=VMEM_LIMIT),
        name="unpack",
    )(gathered)


def mix_kernel(plan, images, partner, weight, stream):
    n, rows = plan.images, plan.rows
    place = lax.broadcasted_iota(jnp.int32, (n, rows), 1)
    own = lax.broadcasted_iota(jnp.int32, (n, rows), 0)
    share_one = weight[...]
    for p in range(PIX):
        pick_own = jnp.where(place == own * PIX + p, 1.0, 0.0).astype(BF16)
        pick_partner = jnp.where(place == partner[...] * PIX + p, 1.0, 0.0).astype(BF16)
        mine = dot(pick_own, images[...])
        theirs = dot(pick_partner, images[...])
        stream[p * n : (p + 1) * n, :] = share_one * mine + (1.0 - share_one) * theirs


def mix(plan, images, partner, mix_weight):
    return pl.pallas_call(
        functools.partial(mix_kernel, plan),
        out_shape=jax.ShapeDtypeStruct((plan.rows, C), F32),
        in_specs=[VM] * 3,
        out_specs=VM,
        compiler_params=pltpu.CompilerParams(vmem_limit_bytes=VMEM_LIMIT),
        name="mix",
    )(
        images.reshape(plan.rows, C),
        partner.reshape(plan.images, 1),
        mix_weight.reshape(plan.images, 1),
    )


def forward_kernel(plan, x, we, wp, wr, wx, small, tail, *refs):
    out, expanded, depth, projected, stat_e, stat_c, pooled, presq, gate = refs[:9]
    x_low, act, sums = refs[9:12]
    ex = exchange_refs(refs[12:], 2 * GROUPS + 1)
    ex_one, ex_two, ex_three = ex[:GROUPS], ex[GROUPS : 2 * GROUPS], ex[2 * GROUPS]
    n = plan.images
    enter(plan)
    x_low[...] = x[...].astype(BF16)
    for g in range(GROUPS):
        cols = slice(g * GW, (g + 1) * GW)

        def expand(m, carry, cols=cols):
            rows = pl.ds(pl.multiple_of(m * MBLK * n, MBLK * n), MBLK * n)
            value = dot(x_low[rows, :], we[:, cols])
            expanded[pl.ds(m * MBLK, MBLK), :, cols] = value.reshape(MBLK, n, GW)
            return (
                carry[0] + jnp.sum(value.reshape(-1, 8, GW), axis=0),
                carry[1] + jnp.sum((value * value).reshape(-1, 8, GW), axis=0),
            )

        zero = jnp.zeros((8, GW), F32)
        s, q = lax.fori_loop(0, PIX // MBLK, expand, (zero, zero))
        if g == 0:
            entered(plan)
        share(plan, *ex_one[g], row_sum(s), row_sum(q))

    def put_sums(j, totals):
        for i, t in enumerate(totals):
            sums[i : i + 1, lanes(j)] = row_sum(t)

    for g in range(GROUPS):
        cols = slice(g * GW, (g + 1) * GW)
        mean, rstd = moments(plan, collect(plan, *ex_one[g]))
        stat_e[0:1, cols] = mean
        stat_e[1:2, cols] = rstd
        scale = rstd * small[9:10, cols]
        stat_e[4:5, cols] = 0.5 * scale
        stat_e[5:6, cols] = 0.5 * (small[10:11, cols] - mean * scale)

        def chunk(j):
            return (
                stat_e[4:5, lanes(j)],
                stat_e[5:6, lanes(j)],
                [small[t : t + 1, lanes(j)] for t in range(9)],
            )

        def spread(j, b, hoisted, totals):
            scale, shift, w = hoisted
            act_one = []
            for p in range(PIX):
                half = expanded[p, images_at(b), lanes(j)] * scale + shift
                act_one.append(half * half_tanh(half) + half)
            made = [None] * PIX
            for o, t, i in TAPS:
                term = act_one[i] * w[t]
                made[o] = term if made[o] is None else made[o] + term
            s, q = totals
            for p in range(PIX):
                depth[p, images_at(b), lanes(j)] = made[p]
                s = s + made[p]
                q = q + made[p] * made[p]
            return s, q

        over_tiles(plan, g * (GW // LANE), GW // LANE, chunk, spread, 2, put_sums)
        share(plan, *ex_two[g], sums[0:1, cols], sums[1:2, cols])

    for g in range(GROUPS):
        cols = slice(g * GW, (g + 1) * GW)
        mean, rstd = moments(plan, collect(plan, *ex_two[g]))
        stat_e[2:3, cols] = mean
        stat_e[3:4, cols] = rstd
        scale = rstd * small[11:12, cols]
        stat_e[6:7, cols] = 0.5 * scale
        stat_e[7:8, cols] = 0.5 * (small[12:13, cols] - mean * scale)

        def chunk_two(j):
            return stat_e[6:7, lanes(j)], stat_e[7:8, lanes(j)]

        def activate(j, b, hoisted, totals):
            scale, shift = hoisted
            total = None
            for p in range(PIX):
                half = depth[p, images_at(b), lanes(j)] * scale + shift
                made = half * half_tanh(half) + half
                act[p, images_at(b), lanes(j)] = made
                total = made if total is None else total + made
            pooled[images_at(b), lanes(j)] = total * (1.0 / PIX)
            return totals

        over_tiles(
            plan, g * (GW // LANE), GW // LANE, chunk_two, activate, 0, lambda j, s: None
        )
    reduced = dot(pooled[...], wr[...], precision=HIGH) + tail[0:1, 0:LANE]
    presq[...] = reduced
    gate[...] = sigmoid(dot(silu(reduced), wx[...], precision=HIGH) + small[13:14, :])

    def project(m, carry):
        rows = pl.ds(pl.multiple_of(m * MBLK * n, MBLK * n), MBLK * n)
        gated = (act[pl.ds(m * MBLK, MBLK), :, :] * gate[...][None]).astype(BF16)
        value = dot(gated.reshape(MBLK * n, E), wp[...])
        projected[rows, :] = value
        return (
            carry[0] + jnp.sum(value.reshape(-1, 8, C), axis=0),
            carry[1] + jnp.sum((value * value).reshape(-1, 8, C), axis=0),
        )

    zero = jnp.zeros((8, C), F32)
    s, q = lax.fori_loop(0, PIX // MBLK, project, (zero, zero))
    share(plan, *ex_three, row_sum(s), row_sum(q))
    mean, rstd = moments(plan, collect(plan, *ex_three))
    stat_c[...] = jnp.zeros((8, C), F32)
    stat_c[0:1, :] = mean
    stat_c[1:2, :] = rstd
    scale = rstd * tail[1:2, :]
    out[...] = x[...] + (projected[...] - mean) * scale + tail[2:3, :]
    for e in ex:
        finish(plan, *e)


def forward(plan, x, weights):
    n = plan.images
    big = (PIX, n, E)
    return pl.pallas_call(
        functools.partial(forward_kernel, plan),
        out_shape=(
            jax.ShapeDtypeStruct((plan.rows, C), F32),
            jax.ShapeDtypeStruct(big, F32),
            jax.ShapeDtypeStruct(big, F32),
            jax.ShapeDtypeStruct((plan.rows, C), F32),
            jax.ShapeDtypeStruct((8, E), F32),
            jax.ShapeDtypeStruct((8, C), F32),
            jax.ShapeDtypeStruct((n, E), F32),
            jax.ShapeDtypeStruct((n, LANE), F32),
            jax.ShapeDtypeStruct((n, E), F32),
        ),
        in_specs=[VM] * 7,
        out_specs=(VM,) * 9,
        scratch_shapes=[
            pltpu.VMEM((plan.rows, C), BF16),
            pltpu.VMEM(big, F32),
            pltpu.VMEM((8, E), F32),
        ]
        + exchange_scratch(plan, [GW] * (2 * GROUPS) + [C]),
        compiler_params=pltpu.CompilerParams(
            collective_id=1, has_side_effects=True, vmem_limit_bytes=VMEM_LIMIT
        ),
        name="layer_forward",
    )(x, *weights)


def head_kernel(plan, x, w_head, bias, label, label_row, partner, weight, *refs):
    grad_x, grad_head, totals_out = refs[:3]
    x_low, turned, hidden, slope, low_grad, pool, stat, sums, gain = refs[3:12]
    hd, n = plan.hd, plan.images
    halves = plan.head_groups
    ng = len(halves)
    ex = exchange_refs(refs[12:], 2 * ng + 1)
    ex_stat, ex_grad, ex_bias = ex[:ng], ex[ng : 2 * ng], ex[2 * ng]
    enter(plan)
    x_low[...] = x[...].astype(BF16)
    turned[...] = x[...].T.astype(BF16)
    gain[...] = w_head[:, C : C + LANE].astype(F32).T[0:8, :]
    for g, (start, width) in enumerate(halves):
        cols = slice(start, start + width)

        def convolve(m, carry, cols=cols, width=width):
            rows = pl.ds(pl.multiple_of(m * MBLK * n, MBLK * n), MBLK * n)
            value = dot(x_low[rows, :], w_head[cols, 0:C], ((1,), (1,)))
            hidden[pl.ds(m * MBLK, MBLK), :, cols] = value.reshape(MBLK, n, width)
            return (
                carry[0] + jnp.sum(value.reshape(-1, 8, width), axis=0),
                carry[1] + jnp.sum((value * value).reshape(-1, 8, width), axis=0),
            )

        zero = jnp.zeros((8, width), F32)
        s, q = lax.fori_loop(0, PIX // MBLK, convolve, (zero, zero))
        if g == 0:
            entered(plan)
        share(plan, *ex_stat[g], row_sum(s), row_sum(q))
    for g, (start, width) in enumerate(halves):
        cols = slice(start, start + width)
        mean, rstd = moments(plan, collect(plan, *ex_stat[g]))
        scale = rstd * gain[0:1, cols]
        stat[0:1, cols] = rstd
        stat[1:2, cols] = -mean * rstd
        stat[2:3, cols] = 0.5 * scale
        stat[3:4, cols] = 0.5 * (gain[1:2, cols] - mean * scale)

        def chunk(j):
            return stat[2:3, lanes(j)], stat[3:4, lanes(j)]

        def activate(j, b, hoisted, totals):
            scale, shift = hoisted
            total = None
            for p in range(PIX):
                half = hidden[p, images_at(b), lanes(j)] * scale + shift
                t = half_tanh(half)
                made = half * t + half
                slope[p, images_at(b), lanes(j)] = (1.0 + t) + half * (1.0 - t * t)
                total = made if total is None else total + made
            pool[images_at(b), lanes(j)] = total * (1.0 / PIX)
            return totals

        over_tiles(plan, start // LANE, width // LANE, chunk, activate, 0, lambda j, s: None)
    pool_low = pool[...].astype(BF16)
    classes = lax.broadcasted_iota(jnp.int32, (n, KP), 1)
    valid = classes < K
    logits = dot(pool_low, w_head[:, C + LANE :]) + bias[...]
    logits = jnp.where(valid, logits, -1e30)
    top = jnp.max(logits, axis=1, keepdims=True)
    lifted = logits - top
    powers = jnp.where(valid, jnp.exp(lifted), 0.0)
    norm = jnp.sum(powers, axis=1, keepdims=True)
    log_probs = lifted - jnp.log(norm)
    picked = lax.broadcasted_iota(jnp.int32, (n, n), 1) == partner[...]
    label_two = jnp.sum(jnp.where(picked, label_row[...], 0), axis=1, keepdims=True)
    w = weight[...]
    targets = w * jnp.where(classes == label[...], 1.0 - SMOOTHING, 0.0) + (1.0 - w) * jnp.where(
        classes == label_two, 1.0 - SMOOTHING, 0.0
    )
    targets = jnp.where(valid, targets + SMOOTHING / K, 0.0)
    loss = -jnp.sum(jnp.where(valid, targets * log_probs, 0.0))
    grad_logits = (powers / norm - targets) * (float(PIX) / plan.count)
    share(plan, *ex_bias, row_sum(grad_logits), jnp.full((1, KP), loss, F32))
    grad_low = grad_logits.astype(BF16)
    pool_grad = dot(grad_low, w_head[:, C + LANE :], ((1,), (1,)))
    pool[...] = pool_grad * (0.5 / PIX)

    def put_sums(j, totals):
        for i, t in enumerate(totals):
            sums[i : i + 1, lanes(j)] = row_sum(t)

    for g, (start, width) in enumerate(halves):
        cols = slice(start, start + width)

        def chunk_back(j):
            return stat[0:1, lanes(j)], stat[1:2, lanes(j)]

        def back(j, b, hoisted, totals):
            rstd, shift = hoisted
            s, q = totals
            flow = pool[images_at(b), lanes(j)]
            for p in range(PIX):
                made = slope[p, images_at(b), lanes(j)] * flow
                slope[p, images_at(b), lanes(j)] = made
                normed = hidden[p, images_at(b), lanes(j)] * rstd + shift
                s = s + made
                q = q + made * normed
            return s, q

        over_tiles(plan, start // LANE, width // LANE, chunk_back, back, 2, put_sums)
        share(plan, *ex_grad[g], sums[0:1, cols], sums[1:2, cols])
    grad_head[:, C + LANE :] = dot(pool_low.T, grad_low).astype(BF16)
    norm_grads = jnp.concatenate(
        [sums[1:2, :], sums[0:1, :], jnp.zeros((LANE - 2, hd), F32)], axis=0
    )
    grad_head[:, C : C + LANE] = norm_grads.T.astype(BF16)
    for g, (start, width) in enumerate(halves):
        cols = slice(start, start + width)
        shift_total, gain_total = collect(plan, *ex_grad[g])
        scale = stat[0:1, cols] * gain[0:1, cols]
        mean_one = shift_total / plan.count
        mean_two = gain_total / plan.count
        stat[4:5, cols] = scale
        stat[5:6, cols] = -scale * stat[0:1, cols] * mean_two
        stat[6:7, cols] = -scale * (mean_one + stat[1:2, cols] * mean_two)
    def into(m, carry):
        rows = pl.ds(pl.multiple_of(m * MBLK * n, MBLK * n), MBLK * n)
        spot = pl.ds(m * MBLK, MBLK)
        value = (
            slope[spot, :, :] * stat[4:5, :] + hidden[spot, :, :] * stat[5:6, :] + stat[6:7, :]
        )
        low = value.reshape(MBLK * n, hd).astype(BF16)
        low_grad[rows, :] = low
        grad_x[rows, :] = dot(low, w_head[:, 0:C])
        return carry

    lax.fori_loop(0, PIX // MBLK, into, 0)
    for at in range(0, hd, LANE):
        part = dot(turned[...], low_grad[:, at : at + LANE])
        grad_head[at : at + LANE, 0:C] = part.T.astype(BF16)
    bias_total, loss_total = collect(plan, *ex_bias)
    totals_out[0:1, :] = bias_total
    totals_out[1:2, :] = loss_total
    for e in ex:
        finish(plan, *e)


def head(plan, x, w_head, bias, labels, partner, mix_weight):
    n, hd = plan.images, plan.hd
    big = (PIX, n, hd)
    widths = [w for _, w in plan.head_groups]
    return pl.pallas_call(
        functools.partial(head_kernel, plan),
        out_shape=(
            jax.ShapeDtypeStruct((plan.rows, C), F32),
            jax.ShapeDtypeStruct((hd, HEAD_W), BF16),
            jax.ShapeDtypeStruct((2, KP), F32),
        ),
        in_specs=[VM] * 7,
        out_specs=(VM,) * 3,
        scratch_shapes=[
            pltpu.VMEM((plan.rows, C), BF16),
            pltpu.VMEM((C, plan.rows), BF16),
            pltpu.VMEM(big, F32),
            pltpu.VMEM(big, F32),
            pltpu.VMEM((plan.rows, hd), BF16),
            pltpu.VMEM((n, hd), F32),
            pltpu.VMEM((8, hd), F32),
            pltpu.VMEM((8, hd), F32),
            pltpu.VMEM((8, hd), F32),
        ]
        + exchange_scratch(plan, widths + widths + [KP]),
        compiler_params=pltpu.CompilerParams(
            collective_id=2, has_side_effects=True, vmem_limit_bytes=VMEM_LIMIT
        ),
        name="head",
    )(
        x,
        w_head,
        bias,
        labels.reshape(n, 1),
        labels.reshape(1, n),
        partner.reshape(n, 1),
        mix_weight.reshape(n, 1),
    )


def backward_kernel(plan, x, grad, expanded, depth, projected, stat_e, stat_c, pooled, presq, gate, we, wp, wr, wx, small, tail, *refs):
    grad_x, packed = refs[:2]
    turned, act, flow, low_proj, gated, sums, coef, squeeze_grad, flat = refs[2:11]
    ex = exchange_refs(refs[11:], 2 * GROUPS + 1)
    ex_two, ex_one, ex_three = ex[:GROUPS], ex[GROUPS : 2 * GROUPS], ex[2 * GROUPS]
    n = plan.images
    lane = lax.broadcasted_iota(jnp.int32, (1, LANE), 1)
    is_low = lane < SQ
    enter(plan)
    mean_c, rstd_c = stat_c[0:1, :], stat_c[1:2, :]
    s = row_sum(jnp.sum(grad[...].reshape(-1, 8, C), axis=0))
    q = row_sum(
        jnp.sum((grad[...] * ((projected[...] - mean_c) * rstd_c)).reshape(-1, 8, C), axis=0)
    )
    entered(plan)
    share(plan, *ex_three, s, q)
    bias_three, gain_three = s, q

    def chunk_two(j):
        return stat_e[6:7, lanes(j)], stat_e[7:8, lanes(j)]

    def activate(j, b, hoisted, totals):
        scale, shift = hoisted
        for p in range(PIX):
            half = depth[p, images_at(b), lanes(j)] * scale + shift
            act[p, images_at(b), lanes(j)] = half * half_tanh(half) + half
        return totals

    over_tiles(plan, 0, NJ, chunk_two, activate, 0, lambda j, s: None)

    def regate(m, carry):
        rows = pl.ds(pl.multiple_of(m * MBLK * n, MBLK * n), MBLK * n)
        value = (act[pl.ds(m * MBLK, MBLK), :, :] * gate[...][None]).astype(BF16)
        gated[rows, :] = value.reshape(MBLK * n, E)
        return carry

    lax.fori_loop(0, PIX // MBLK, regate, 0)
    turned[...] = x[...].T.astype(BF16)

    bias_total, gain_total = collect(plan, *ex_three)
    scale = rstd_c * tail[1:2, :]
    mean_one, mean_two = bias_total / plan.count, gain_total / plan.count
    low_proj[...] = (
        scale
        * (grad[...] - mean_one - (projected[...] - mean_c) * (rstd_c * mean_two))
    ).astype(BF16)

    def into_gated(m, carry):
        rows = pl.ds(pl.multiple_of(m * MBLK * n, MBLK * n), MBLK * n)
        value = dot(low_proj[rows, :], wp[...], ((1,), (1,)))
        flow[pl.ds(m * MBLK, MBLK), :, :] = value.reshape(MBLK, n, E)
        return carry

    lax.fori_loop(0, PIX // MBLK, into_gated, 0)

    def gate_back(j, b, hoisted, totals):
        total = None
        for p in range(PIX):
            term = flow[p, images_at(b), lanes(j)] * act[p, images_at(b), lanes(j)]
            total = term if total is None else total + term
        opened = gate[images_at(b), lanes(j)]
        squeeze_grad[images_at(b), lanes(j)] = total * opened * (1.0 - opened)
        return totals

    over_tiles(plan, 0, NJ, lambda j: None, gate_back, 0, lambda j, s: None)
    excite_grad = squeeze_grad[...]
    sums[13:14, :] = row_sum(excite_grad)
    squeezed = silu(presq[...])
    presq_grad = dot(excite_grad, wx[...], ((1,), (1,)), HIGH) * silu_slope(presq[...])
    grad_wx = dot(squeezed.T, excite_grad, precision=HIGH)
    for j in range(NJ):
        flat[pl.ds(ROW_X + j, SQ, stride=NJ), :] = grad_wx[0:SQ, j * LANE : (j + 1) * LANE]
    grad_reduce_b = row_sum(presq_grad)
    grad_wr = dot(pooled[...].T, presq_grad, precision=HIGH)
    squeeze_grad[...] = dot(presq_grad, wr[...], ((1,), (1,)), HIGH) * (1.0 / PIX)

    def put_sums(first_row):
        def put(j, totals):
            for i, t in enumerate(totals):
                sums[first_row + i : first_row + i + 1, lanes(j)] = row_sum(t)

        return put

    def chunk_norm(j):
        return (
            stat_e[6:7, lanes(j)],
            stat_e[7:8, lanes(j)],
            stat_e[2:3, lanes(j)],
            stat_e[3:4, lanes(j)],
        )

    def back_two(j, b, hoisted, totals):
        scale, shift, mean, rstd = hoisted
        gain_sum, bias_sum = totals
        opened = gate[images_at(b), lanes(j)] * 0.5
        pool_flow = squeeze_grad[images_at(b), lanes(j)] * 0.5
        for p in range(PIX):
            value = depth[p, images_at(b), lanes(j)]
            half = value * scale + shift
            t = half_tanh(half)
            made = (flow[p, images_at(b), lanes(j)] * opened + pool_flow) * (
                (1.0 + t) + half * (1.0 - t * t)
            )
            flow[p, images_at(b), lanes(j)] = made
            bias_sum = bias_sum + made
            gain_sum = gain_sum + made * ((value - mean) * rstd)
        return gain_sum, bias_sum

    for g in range(GROUPS):
        cols = slice(g * GW, (g + 1) * GW)
        over_tiles(plan, g * (GW // LANE), GW // LANE, chunk_norm, back_two, 2, put_sums(11))
        share(plan, *ex_two[g], sums[12:13, cols], sums[11:12, cols])

    proj_turned = low_proj[...].astype(F32).T.astype(BF16)
    for j in range(NJ):
        part = dot(proj_turned, gated[:, j * LANE : (j + 1) * LANE])
        for h in range(C // LANE):
            flat[pl.ds(ROW_P + 2 * j * LANE + h, LANE, stride=2), :] = part[
                h * LANE : (h + 1) * LANE, :
            ].T

    def norm_coefs(g, pair, row, stat_row, gain_row):
        cols = slice(g * GW, (g + 1) * GW)
        mean, rstd = stat_e[stat_row : stat_row + 1, cols], stat_e[stat_row + 1 : stat_row + 2, cols]
        scale = rstd * small[gain_row : gain_row + 1, cols]
        mean_one, mean_two = pair[0] / plan.count, pair[1] / plan.count
        coef[row : row + 1, cols] = scale
        coef[row + 1 : row + 2, cols] = -scale * rstd * mean_two
        coef[row + 2 : row + 3, cols] = -scale * (mean_one - mean * rstd * mean_two)

    def chunk_one(j):
        return (
            [coef[i : i + 1, lanes(j)] for i in range(3)],
            [small[t : t + 1, lanes(j)] for t in range(9)],
            [stat_e[i : i + 1, lanes(j)] for i in (4, 5, 0, 1)],
        )

    def back_one(j, b, hoisted, totals):
        (c_flow, c_value, c_const), w, (scale, shift, mean, rstd) = hoisted
        w_sums, gain_sum, bias_sum = list(totals[:9]), totals[9], totals[10]
        spread_grad = []
        for p in range(PIX):
            spread_grad.append(
                flow[p, images_at(b), lanes(j)] * c_flow
                + (depth[p, images_at(b), lanes(j)] * c_value + c_const)
            )
        act_one = []
        for p in range(PIX):
            half = expanded[p, images_at(b), lanes(j)] * scale + shift
            t = half_tanh(half)
            act_one.append(half * t + half)
        made = [None] * PIX
        for o, t, i in TAPS:
            w_sums[t] = w_sums[t] + spread_grad[o] * act_one[i]
            term = spread_grad[o] * w[t]
            made[i] = term if made[i] is None else made[i] + term
        for p in range(PIX):
            value = expanded[p, images_at(b), lanes(j)]
            half = value * scale + shift
            t = half_tanh(half)
            result = made[p] * (0.5 * ((1.0 + t) + half * (1.0 - t * t)))
            flow[p, images_at(b), lanes(j)] = result
            bias_sum = bias_sum + result
            gain_sum = gain_sum + result * ((value - mean) * rstd)
        return tuple(w_sums) + (gain_sum, bias_sum)

    for g in range(GROUPS):
        cols = slice(g * GW, (g + 1) * GW)
        norm_coefs(g, collect(plan, *ex_two[g]), 0, 2, 11)
        over_tiles(plan, g * (GW // LANE), GW // LANE, chunk_one, back_one, 11, put_sums(0))
        share(plan, *ex_one[g], sums[10:11, cols], sums[9:10, cols])

    for j in range(NJ):
        flat[pl.ds(ROW_D + j, 14, stride=NJ), :] = sums[0:14, j * LANE : (j + 1) * LANE]
    pair_buf = refs[11 + 3 * (2 * GROUPS + 1)]
    pair_buf[...] = grad_wr
    evens = pair_buf[pl.ds(0, E // 2, stride=2), :]
    odds = pair_buf[pl.ds(1, E // 2, stride=2), :]
    flat[ROW_R:ROW_X, :] = jnp.where(is_low, evens, pltpu.roll(odds, SQ, 1))

    def turn(row):
        return pltpu.roll(jnp.broadcast_to(row, (8, LANE)), SQ, 1)[0:1, :]

    pieces = [turn(v[:, h * LANE : (h + 1) * LANE]) for v in (gain_three, bias_three) for h in (0, 1)]
    flat[ROW_S : ROW_S + 1, :] = jnp.where(is_low, grad_reduce_b, pieces[0])
    for i in range(3):
        flat[ROW_S + 1 + i : ROW_S + 2 + i, :] = jnp.where(is_low, pieces[i], pieces[i + 1])
    flat[ROW_S + 4 : ROW_S + 5, :] = pieces[3]

    grad_x[...] = grad[...]
    for g in range(GROUPS):
        cols = slice(g * GW, (g + 1) * GW)
        norm_coefs(g, collect(plan, *ex_one[g]), 0, 0, 9)

        def into(m, carry, cols=cols):
            rows = pl.ds(pl.multiple_of(m * MBLK * n, MBLK * n), MBLK * n)
            spot = pl.ds(m * MBLK, MBLK)
            value = (
                flow[spot, :, cols] * coef[0:1, cols]
                + expanded[spot, :, cols] * coef[1:2, cols]
                + coef[2:3, cols]
            )
            low = value.reshape(MBLK * n, GW).astype(BF16)
            gated[rows, cols] = low
            grad_x[rows, :] += dot(low, we[:, cols], ((1,), (1,)))
            return carry

        lax.fori_loop(0, PIX // MBLK, into, 0)
        for j in range(g * (GW // LANE), (g + 1) * (GW // LANE)):
            flat[pl.ds(j, C, stride=NJ), :] = dot(
                turned[...], gated[:, j * LANE : (j + 1) * LANE]
            )
    for f in range(plan.nf):
        packed[f * plan.chunk : (f + 1) * plan.chunk, :] = flat[
            plan.base[f] : plan.base[f] + plan.chunk, :
        ].astype(BF16)
    for e in ex:
        finish(plan, *e)


def backward(plan, x, grad, kept, weights):
    n = plan.images
    big = (PIX, n, E)
    return pl.pallas_call(
        functools.partial(backward_kernel, plan),
        out_shape=(
            jax.ShapeDtypeStruct((plan.rows, C), F32),
            jax.ShapeDtypeStruct((plan.nf * plan.chunk, LANE), BF16),
        ),
        in_specs=[VM] * 16,
        out_specs=(VM,) * 2,
        scratch_shapes=[
            pltpu.VMEM((C, plan.rows), BF16),
            pltpu.VMEM(big, F32),
            pltpu.VMEM(big, F32),
            pltpu.VMEM((plan.rows, C), BF16),
            pltpu.VMEM((plan.rows, E), BF16),
            pltpu.VMEM((16, E), F32),
            pltpu.VMEM((8, E), F32),
            pltpu.VMEM((n, E), F32),
            pltpu.VMEM((plan.flat, LANE), F32),
        ]
        + exchange_scratch(plan, [GW] * (2 * GROUPS) + [C])
        + [pltpu.VMEM((E, LANE), F32)],
        compiler_params=pltpu.CompilerParams(
            collective_id=3, has_side_effects=True, vmem_limit_bytes=VMEM_LIMIT
        ),
        name="layer_backward",
    )(x, grad, *kept, *weights)


def adam_update(master, first, second, average, grad):
    first_new = BETA_ONE * first + (1.0 - BETA_ONE) * grad
    second_new = BETA_TWO * second + (1.0 - BETA_TWO) * grad * grad
    fix_one = 1.0 - BETA_ONE**STEP
    fix_two = 1.0 - BETA_TWO**STEP
    master_new = master * (1.0 - RATE * DECAY_WEIGHT) - RATE * (first_new / fix_one) / (
        jnp.sqrt(second_new / fix_two) + EPS_ADAM
    )
    average_new = EMA_RATE * average + (1.0 - EMA_RATE) * master_new
    return (master_new, first_new, second_new, average_new)


def on_device(mesh, images, partner, mix_weight, labels, *states):
    block, head_state, bias_state = states[0:4], states[4:8], states[8:12]
    row = C + 2 + K
    plan = Plan(mesh, images.shape[0], head_state[0].shape[0] // row)
    half = (plan.hd // LANE + 1) // 2 * LANE
    plan.head_groups = [(0, half), (half, plan.hd - half)]
    start = lax.axis_index("fsdp") * plan.shard
    offset = start - start // (16 * LANE) * (16 * LANE)
    weights = []
    for layer in range(LAYERS):
        flat = lax.dynamic_update_slice(
            jnp.zeros((plan.chunk * LANE,), BF16), block[0][layer].astype(BF16), (offset,)
        )
        gathered = lax.all_gather(flat.reshape(plan.chunk, LANE), "fsdp", axis=0, tiled=True)
        weights.append(unpack(plan, gathered))
    grid = head_state[0].astype(BF16).reshape(plan.head_rows, row)
    grid = jnp.concatenate(
        [
            grid[:, : C + 2],
            jnp.zeros((plan.head_rows, LANE - 2), BF16),
            grid[:, C + 2 :],
            jnp.zeros((plan.head_rows, KP - K), BF16),
        ],
        axis=1,
    )
    grid = jnp.pad(grid, ((0, plan.head_pad - plan.head_rows), (0, 0)))
    w_head = lax.all_gather(grid, "fsdp", axis=0, tiled=True)
    bias = jnp.pad(bias_state[0], (0, KP - K)).reshape(1, KP)

    stream = mix(plan, images, partner, mix_weight)
    inputs, kept = [], []
    for layer in range(LAYERS):
        inputs.append(stream)
        made = forward(plan, stream, weights[layer])
        stream = made[0]
        kept.append(made[1:])
    grad, head_grad, totals = head(plan, stream, w_head, bias, labels, partner, mix_weight)
    loss_sum = totals[1, 0]
    grad_bias = totals[0, :K]
    head_grad = lax.psum_scatter(head_grad, "fsdp", scatter_dimension=0, tiled=True)
    block_grads = [None] * LAYERS
    for layer in reversed(range(LAYERS)):
        grad, packed = backward(plan, inputs[layer], grad, kept[layer], weights[layer])
        block_grads[layer] = lax.psum_scatter(packed, "fsdp", scatter_dimension=0, tiled=True)
    block_grad, head_grad = lax.psum((jnp.stack(block_grads), head_grad), "dp")
    block_grad = lax.dynamic_slice(
        block_grad.reshape(LAYERS, plan.chunk * LANE), (0, offset), (LAYERS, plan.shard)
    ).astype(F32)
    head_grad = head_grad[: plan.head_rows].astype(F32)
    head_grad = jnp.concatenate(
        [head_grad[:, : C + 2], head_grad[:, C + LANE : C + LANE + K]], axis=1
    ).reshape(-1)
    return (
        (loss_sum,)
        + adam_update(*block, block_grad)
        + adam_update(*head_state, head_grad)
        + adam_update(*bias_state, grad_bias)
    )


def solution(mesh):
    data = P(("dp", "fsdp"))
    states = (P(None, "fsdp"),) * 4 + (P("fsdp"),) * 4 + (P(),) * 4
    return jax.shard_map(
        functools.partial(on_device, mesh),
        mesh=mesh,
        in_specs=(P(("dp", "fsdp"), None, None), data, data, data) + states,
        out_specs=(P(),) + states,
        check_vma=False,
    )
```

time: 2350 us -> 660 us (0.28)
  blocking collectives: 806 us -> 0 us
  other arithmetic: 492 us -> 14.3 us
  local copies, waits for them, and re-layouts: 468 us -> 23.4 us
  Pallas kernels: 0 us -> 370 us
  waiting for transfers between devices: 443 us -> 229 us
  matrix products: 102 us -> 0 us
    psum x20 -> x0, blocking collectives: 806 us -> none  [the longest x10 402 us: norm_stats(): lax.psum((jnp.sum(values_in, axis=(0, 1)), jnp.sum(values_in * values_in,...]
    unnamed x5 -> x9, waiting for transfers between devices: 385 us -> 2.01 us
    pallas_call x0 -> x11, Pallas kernels: none -> 370 us  [the longest x3 168 us: backward(): pl.pallas_call(functools.partial(backward_kernel, plan), out_shape=(jax.S...]
    reduce_sum x25 -> x0, other arithmetic: 308 us -> none  [the longest x6 146 us: depthwise(): padded[:, tap_row:tap_row + SIDE, tap_col:tap_col + SIDE, :]]
    reduce_scatter x0 -> x4, waiting for transfers between devices: none -> 151 us  [the longest x3 108 us: on_device(): lax.psum_scatter(packed, 'fsdp', scatter_dimension=0, tiled=True)]
    reshape x43 -> x5, local copies, waits for them, and re-layouts: 142 us -> 3.39 us  [the longest x1 0.82 us: on_device(): grid = head_state[0].astype(BF16).reshape(plan.head_rows, row)]
    concatenate x5 -> x1, local copies, waits for them, and re-layouts: 110 us -> 0.89 us  [on_device(): jnp.concatenate([grid[:, :C + 2], jnp.zeros((plan.head_rows, LANE - 2), B...]
    unnamed x491 -> x35, local copies, waits for them, and re-layouts: 110 us -> 4.49 us
  transfers between devices with their start and end apart: 3 -> 9, of which waited for: 3 -> 6; matrix products, arithmetic and copies ran while one was open for 0% -> 2% of each run, Pallas kernels for 0% -> 25%
where the time goes in v1:
time: 660 us; the launch traced here: 652 us
  Pallas kernels  370 us (56%)
  waiting for transfers between devices  229 us (35%)
  local copies, waits for them, and re-layouts  23.4 us (4%)
  between operations  14.7 us (2%)
  other arithmetic  14.3 us (2%)
    pallas_call x3, Pallas kernels, backward(): pl.pallas_call(functools.partial(backward_kernel, plan), out_shape=(jax.S...  168 us
    pallas_call x3, Pallas kernels, forward(): pl.pallas_call(functools.partial(forward_kernel, plan), out_shape=(jax.Sh...  149 us
    reduce_scatter x3, waiting for transfers between devices, on_device(): lax.psum_scatter(packed, 'fsdp', scatter_dimension=0, tiled=True)  108 us
    psum x1, waiting for transfers between devices, on_device(): block_grad, head_grad = lax.psum((jnp.stack(block_grads), head_grad), 'dp')  61.1 us
    reduce_scatter x1, waiting for transfers between devices, on_device(): lax.psum_scatter(head_grad, 'fsdp', scatter_dimension=0, tiled=True)  42.5 us
    pallas_call x1, Pallas kernels, head(): pl.pallas_call(functools.partial(head_kernel, plan), out_shape=(jax.Shape...  37.6 us
    all_gather x3, waiting for transfers between devices, on_device(): lax.all_gather(flat.reshape(plan.chunk, LANE), 'fsdp', axis=0, tiled=True)  15.4 us
  transfers between devices with their start and end apart: 9, of which 6 were waited for; matrix products, arithmetic and copies ran while one was open for 2% of the time, Pallas kernels for 25%

profile of v1, /device:TPU:0, one launch (start us, length us, event | category | flops | bytes accessed | tf_op | source)
XLA Modules:
  0.0 652.3 jit_solution(11776825513626970925)
XLA Ops:
  7.2 1.9 convert.5
  9.2 4.2 slice_reduce_fusion
  13.4 2.4 dynamic_update_slice.9
  16.5 2.4 dynamic_update_slice.10
  19.7 2.4 dynamic_update_slice.11
  22.1 0.7 copy-done.6
  23.0 0.8 reshape.73
  24.1 0.9 concatenate.6
  25.7 0.7 copy.30.weight
  27.7 5.1 mix.1.x
  32.8 15.3 %all-gather.5.cloned.1.call-done.got = bf16[8064,128]{1,0:T(8,128)(2,1)} async-done(((bf16[1008,128]{1,0:T(8,128)(2,1)}), bf16[8064,128]{1,0:T(8,128)(2,1)}) %all-gather.5.cloned.1.call-update) | async-done | bytes 2064400 | tf_op jit(solution)/shard_map/all_gather | solution.py:884
  48.1 3.6 unpack.3
  51.8 57.3 %layer_forward.3 = (f32[1024,256]{1,0:T(8,128)}, f32[16,64,1536]{2,1,0:T(8,128)}, f32[16,64,1536]{2,1,0:T(8,128)}, f32[1024,256]{1,0:T(8,128)}, f32[8,1536]{1,0:...) custom-call(f32[1024,256]{1,0:T(8,128)} %mix.1.x, ...), custom_call_target="tpu_custom_call" | custom-call | tf_op jit(solution)/shard_map/layer_forward/pallas_call | solution.py:402
  109.1 3.6 unpack.4
  112.7 45.7 %layer_forward.4 = (f32[1024,256]{1,0:T(8,128)}, f32[16,64,1536]{2,1,0:T(8,128)}, f32[16,64,1536]{2,1,0:T(8,128)}, f32[1024,256]{1,0:T(8,128)}, f32[8,1536]{1,0:...) custom-call(f32[1024,256]{1,0:T(8,128)} %get-tuple-element.72.x, ...), custom_call_target="tpu_custom_call" | custom-call | tf_op jit(solution)/shard_map/layer_forward/pallas_call | solution.py:402
  158.4 3.6 unpack.5
  162.1 46.3 %layer_forward.5 = (f32[1024,256]{1,0:T(8,128)}, f32[16,64,1536]{2,1,0:T(8,128)}, f32[16,64,1536]{2,1,0:T(8,128)}, f32[1024,256]{1,0:T(8,128)}, f32[8,1536]{1,0:...) custom-call(f32[1024,256]{1,0:T(8,128)} %get-tuple-element.79.x, ...), custom_call_target="tpu_custom_call" | custom-call | tf_op jit(solution)/shard_map/layer_forward/pallas_call | solution.py:402
  208.4 37.6 %head.1 = (f32[1024,256]{1,0:T(8,128)}, bf16[1280,1408]{1,0:T(8,128)(2,1)}, f32[2,1024]{1,0:T(2,128)}) custom-call(f32[1024,256]{1,0:T(8,128)} %get-tuple-element.86.x, bf16[1280,1408]{1,0:T(8,128)(2,1)} %all-gather.11.cloned.1.call-done.w_head, f32[1,1024]{1,0:T(1,128)} %bitcast.28, s32[64,1]{1,0:T(8,128)} %copy.31.label, s32[1,64]{1,0:T(1,128)} %bitcast.29, ...), custom_call_target="tpu_custom_call" | custom-call | tf_op jit(solution)/shard_map/head/pallas_call | solution.py:572
  246.1 56.0 %layer_backward.3 = (f32[1024,256]{1,0:T(8,128)}, bf16[8064,128]{1,0:T(8,128)(2,1)}) custom-call(f32[1024,256]{1,0:T(8,128)} %get-tuple-element.79.x, f32[1024,256]{1,0:T(8,128)} %get-tuple-element.88.grad, f32[16,64,1536]{2,1,0:T(8,128)} %get-tuple-element.89.expanded, f32[16,64,1536]{2,1,0:T(8,128)} %get-tuple-element.90.depth, ...), custom_call_target="tpu_custom_call" | custom-call | tf_op jit(solution)/shard_map/layer_backward/pallas_call | solution.py:831
  302.1 56.7 %layer_backward.4 = (f32[1024,256]{1,0:T(8,128)}, bf16[8064,128]{1,0:T(8,128)(2,1)}) custom-call(f32[1024,256]{1,0:T(8,128)} %get-tuple-element.72.x, f32[1024,256]{1,0:T(8,128)} %get-tuple-element.97.grad, f32[16,64,1536]{2,1,0:T(8,128)} %get-tuple-element.98.expanded, f32[16,64,1536]{2,1,0:T(8,128)} %get-tuple-element.99.depth, ...), custom_call_target="tpu_custom_call" | custom-call | tf_op jit(solution)/shard_map/layer_backward/pallas_call | solution.py:831
  358.9 54.8 %layer_backward.5 = (f32[1024,256]{1,0:T(8,128)}, bf16[8064,128]{1,0:T(8,128)(2,1)}) custom-call(f32[1024,256]{1,0:T(8,128)} %mix.1.x, f32[1024,256]{1,0:T(8,128)} %get-tuple-element.106.grad, f32[16,64,1536]{2,1,0:T(8,128)} %get-tuple-element.107.expanded, f32[16,64,1536]{2,1,0:T(8,128)} %get-tuple-element.108.depth, ...), custom_call_target="tpu_custom_call" | custom-call | tf_op jit(solution)/shard_map/layer_backward/pallas_call | solution.py:831
  415.8 34.9 %reduce-scatter.5.cloned.1.call-done = bf16[1008,128]{1,0:T(8,128)(2,1)} async-done(((bf16[8064,128]{1,0:T(8,128)(2,1)}), bf16[1008,128]{1,0:T(8,128)(2,1)}) %reduce-scatter.5.cloned.1.call-update) | async-done | bytes 258064 | tf_op jit(solution)/shard_map/reduce_scatter | solution.py:914
  450.7 36.4 %reduce-scatter.7.cloned.1.call-done = bf16[1008,128]{1,0:T(8,128)(2,1)} async-done(((bf16[8064,128]{1,0:T(8,128)(2,1)}), bf16[1008,128]{1,0:T(8,128)(2,1)}) %reduce-scatter.7.cloned.1.call-update) | async-done | bytes 258064 | tf_op jit(solution)/shard_map/reduce_scatter | solution.py:914
  487.0 36.8 %reduce-scatter.9.cloned.1.call-done = bf16[1008,128]{1,0:T(8,128)(2,1)} async-done(((bf16[8064,128]{1,0:T(8,128)(2,1)}), bf16[1008,128]{1,0:T(8,128)(2,1)}) %reduce-scatter.9.cloned.1.call-update) | async-done | bytes 258064 | tf_op jit(solution)/shard_map/reduce_scatter | solution.py:914
  523.8 1.3 maximum_bitcast_fusion
  525.1 1.4 copy.36
  526.5 42.5 %reduce-scatter.11.cloned.1.call-done = bf16[160,1408]{1,0:T(8,128)(2,1)} async-done(((bf16[1280,1408]{1,0:T(8,128)(2,1)}), bf16[160,1408]{1,0:T(8,128)(2,1)}) %reduce-scatter.11.cloned.1.call-update) | async-done | bytes 450576 | tf_op jit(solution)/shard_map/reduce_scatter | solution.py:910
  570.2 61.1 %all-reduce.4.cloned.1.call-done = (bf16[3,129024]{1,0:T(4,128)(2,1)}, bf16[160,1408]{1,0:T(8,128)(2,1)}) async-done(((bf16[3,129024]{1,0:T(4,128)(2,1)}, bf16[160,1408]{1,0:T(8,128)(2,1)}), (bf16[3,129024]{1,0:T(4,128)(2,1)}, bf16[160,1408]{1,0:T(8,128)(2,1)})) %all-reduce.4.cloned.1.call-update) | async-done | bytes 1224720 | tf_op jit(solution)/shard_map/psum | solution.py:915
  631.3 0.9 slice.44
  632.3 1.1 slice.45
  634.2 3.7 add_multiply_fusion.1
  638.8 6.5 %add_multiply_fusion = (f32[3,125640]{1,0:T(4,128)}, f32[3,125640]{1,0:T(4,128)}, f32[3,125640]{1,0:T(4,128)}, f32[3,125640]{1,0:T(4,128)}) fusion(f32[3,125640]{1,0:T(4,128)S(1)} %copy-done.2, f32[3,125640]{1,0:T(4,128)S(1)} %copy-done, bf16[3,129024]{1,0:T(4,128)(2,1)S(1)} %copy-done.7, s32[]{:T(128)S(6)} %select_n.12, f32[3,125640]{1,0:T(4,128)S(1)} %copy-done.3, ...), kind=kLoop, calls=%fused_computation.3 | loop fusion | flops 5653800 | bytes 12815284 | tf_op jit(solution)/shard_map/add | solution.py:867
  (70 shorter events, 9.0 us)
Async XLA Ops:
  7.2 41.0 %all-gather.5.cloned.1.call-start = ((), (), s32[]{:S(2)}) async-start(), calls=%async_computation.4 | async-start | bytes 2322432 | tf_op jit(solution)/shard_map/all_gather | solution.py:884
  13.3 9.6 %copy-start.1 = (f32[201280]{0:T(1024)S(1)}, f32[201280]{0:T(1024)}, u32[]{:S(2)}) copy-start(f32[201280]{0:T(1024)} %param.24) | copy-start | bytes 2415364
  15.7 0.7 copy-start.4
  16.5 92.6 %all-gather.7.cloned.1.call-start = ((), (), s32[]{:S(2)}) async-start(), calls=%async_computation.5 | async-start | bytes 2322432 | tf_op jit(solution)/shard_map/all_gather | solution.py:884
  18.9 0.7 copy-start.5
  19.6 138.8 %all-gather.9.cloned.1.call-start = ((), (), s32[]{:S(2)}) async-start(), calls=%async_computation.6 | async-start | bytes 2322432 | tf_op jit(solution)/shard_map/all_gather | solution.py:884
  22.1 0.7 copy-start.6
  22.9 2.2 copy-start.15
  22.9 2.9 copy-start.16
  22.9 3.6 copy-start.13
  22.9 4.2 copy-start.9
  22.9 185.5 %all-gather.11.cloned.1.call-start = ((), (), s32[]{:S(2)}) async-start(), calls=%async_computation.7 | async-start | bytes 4055040 | tf_op jit(solution)/shard_map/all_gather | solution.py:897
  25.0 425.7 %reduce-scatter.5.cloned.1.call-start = ((), (), s32[]{:S(2)}) async-start(), calls=%async_computation.8 | async-start | bytes 2322432 | tf_op jit(solution)/shard_map/reduce_scatter | solution.py:914
  413.7 73.3 %reduce-scatter.7.cloned.1.call-start = ((), (), s32[]{:S(2)}) async-start(), calls=%async_computation.9 | async-start | bytes 2322432 | tf_op jit(solution)/shard_map/reduce_scatter | solution.py:914
  414.3 109.6 %reduce-scatter.9.cloned.1.call-start = ((), (), s32[]{:S(2)}) async-start(), calls=%async_computation.10 | async-start | bytes 2322432 | tf_op jit(solution)/shard_map/reduce_scatter | solution.py:914
  415.0 154.0 %reduce-scatter.11.cloned.1.call-start = ((), (), s32[]{:S(2)}) async-start(), calls=%async_computation.11 | async-start | bytes 4055040 | tf_op jit(solution)/shard_map/reduce_scatter | solution.py:910
  415.8 215.6 %all-reduce.4.cloned.1.call-start = ((), (), s32[]{:S(2)}) async-start(), calls=%async_computation.12 | async-start | bytes 2965504 | tf_op jit(solution)/shard_map/psum | solution.py:915
  525.1 44.0 %copy-start.14 = (f32[2,1024]{1,0:T(2,128)S(1)}, f32[2,1024]{1,0:T(2,128)}, u32[]{:S(2)}) copy-start(f32[2,1024]{1,0:T(2,128)} %get-tuple-element.87) | copy-start | bytes 24580
  525.1 44.5 %copy-start.10 = (f32[1000]{0:T(1024)S(1)}, f32[1000]{0:T(1024)}, u32[]{:S(2)}) copy-start(f32[1000]{0:T(1024)} %param.31) | copy-start | bytes 12004
  525.1 44.5 %copy-start.11 = (f32[1000]{0:T(1024)S(1)}, f32[1000]{0:T(1024)}, u32[]{:S(2)}) copy-start(f32[1000]{0:T(1024)} %param.29) | copy-start | bytes 12004
  525.1 44.5 %copy-start.12 = (f32[1000]{0:T(1024)S(1)}, f32[1000]{0:T(1024)}, u32[]{:S(2)}) copy-start(f32[1000]{0:T(1024)} %param.30) | copy-start | bytes 12004
  632.3 1.8 copy-start.8
  634.1 3.7 copy-start
  634.1 3.7 copy-start.2
  634.1 4.1 copy-start.3
  634.1 4.6 copy-start.7
Sparse Core Ops, SparseCore 0:
  16.6 31.5 all-gather.4
  50.4 45.1 all-gather.6
  97.2 32.2 all-gather.8
  131.0 50.6 all-gather.10
  413.8 36.8 reduce-scatter.4
  452.8 34.1 reduce-scatter.6
  489.3 34.4 reduce-scatter.8
  526.1 42.8 reduce-scatter.10
  573.2 58.1 all-reduce.3

commit v2 on v1

--- a/solution.py
+++ b/solution.py
@@ -42,7 +42,7 @@
 F32 = jnp.float32
 BF16 = jnp.bfloat16
 HIGH = lax.Precision.HIGHEST
-VMEM_LIMIT = 60 * 1024 * 1024
+VMEM_LIMIT = 63 * 1024 * 1024
 VM = pl.BlockSpec(memory_space=pltpu.VMEM)
 
 
@@ -60,11 +60,26 @@
         self.count = float(self.rows * self.devices)
         self.shard = PB // self.nf
         self.base = [(self.shard * f // LANE) // 16 * 16 for f in range(self.nf)]
-        self.chunk = ceil_to(-(-self.shard // LANE) + 17, 16)
+        self.chunk = ceil_to(-(-self.shard // LANE) + 17, 16 * self.nd)
         self.flat = self.base[-1] + self.chunk
         self.head_pad = ceil_to(head_rows, 16)
         self.hd = self.head_pad * self.nf
         self.head_rows = head_rows
+        self.head_part = ceil_to(-(-head_rows // self.nd), 16)
+        self.head_flat = self.head_pad * (self.nf - 1) + self.head_part * self.nd
+        self.depth = self.nf // 2
+
+    def layer_unit(self):
+        return Unit(self, LANE, self.chunk // self.nd, self.flat, lambda f: self.shard * f // (16 * LANE) * 16)
+
+    def head_unit(self):
+        return Unit(self, HEAD_W, self.head_part, self.head_flat, lambda f: self.head_pad * f)
+
+
+class Unit:
+    def __init__(self, plan, width, part, rows, base):
+        self.plan, self.width, self.part, self.rows, self.base = plan, width, part, rows, base
+        self.owned = part * plan.nd
 
 
 def dot(a, b, dims=((1,), (0,)), precision=None):
@@ -99,8 +114,11 @@
 
 
 def share(plan, buf, send, recv, first, second):
-    buf[0, 0:1, :] = first
-    buf[0, 1:2, :] = second
+    half = buf.shape[1] // 2
+    for r in range(half):
+        cols = slice(r * LANE, (r + 1) * LANE)
+        buf[0, r : r + 1, :] = first[:, cols]
+        buf[0, half + r : half + r + 1, :] = second[:, cols]
 
     def push(step, carry):
         pltpu.make_async_remote_copy(
@@ -120,7 +138,9 @@
     others = buf.at[pl.ds(1, plan.devices - 1)]
     pltpu.make_async_copy(others, others, recv).wait()
     total = jnp.sum(buf[...], axis=0)
-    return total[0:1, :], total[1:2, :]
+    rows = [total[r : r + 1, :] for r in range(buf.shape[1])]
+    half = len(rows) // 2
+    return jnp.concatenate(rows[:half], axis=1), jnp.concatenate(rows[half:], axis=1)
 
 
 def finish(plan, buf, send, recv):
@@ -129,7 +149,7 @@
 
 
 def exchange_scratch(plan, widths):
-    shapes = [pltpu.VMEM((plan.devices, 2, w), F32) for w in widths]
+    shapes = [pltpu.VMEM((plan.devices, 2 * w // LANE, LANE), F32) for w in widths]
     sems = [pltpu.SemaphoreType.DMA(()) for w in widths]
     return shapes + sems + sems
 
@@ -141,6 +161,132 @@
 def moments(plan, pair):
     mean = pair[0] / plan.count
     return mean, lax.rsqrt(pair[1] / plan.count - mean * mean + EPS_NORM)
+
+
+class Reduction:
+    def __init__(self, unit, source, result, refs):
+        self.unit, self.source, self.result = unit, source, result
+        self.got_core, self.sum_core, self.got_dp, self.sum_dp, self.got_rest = refs[:5]
+        self.send, self.recv = refs[5:9], refs[9:13]
+        plan = unit.plan
+        self.dp, self.fs = lax.axis_index("dp"), lax.axis_index("fsdp")
+        self.core, self.deep = lax.rem(self.fs, 2), self.fs // 2
+        self.nd, self.nz = plan.nd, plan.depth
+
+    @staticmethod
+    def scratch(unit):
+        plan = unit.plan
+        nd, nz, w, part = plan.nd, plan.depth, unit.width, unit.part
+        return [
+            pltpu.VMEM((nz, nd, part, w), BF16),
+            pltpu.VMEM((nd, nz, part, w), BF16),
+            pltpu.VMEM((nd - 1, nz, part, w), BF16),
+            pltpu.VMEM((nz, part, w), BF16),
+            pltpu.VMEM((nz - 1, part, w), BF16),
+        ] + [pltpu.SemaphoreType.DMA(())] * 8
+
+    def push(self, stage, source, target, device):
+        pltpu.make_async_remote_copy(
+            src_ref=source,
+            dst_ref=target,
+            send_sem=self.send[stage],
+            recv_sem=self.recv[stage],
+            device_id=device,
+            device_id_type=MESH,
+        ).start()
+
+    def rows_of(self, f, d=0):
+        return pl.multiple_of(self.unit.base(f) + d * self.unit.part, 16)
+
+    def start_core(self):
+        def go(z, carry):
+            for d in range(self.nd):
+                self.push(
+                    0,
+                    self.source.at[pl.ds(self.rows_of(2 * z + 1 - self.core, d), self.unit.part)],
+                    self.got_core.at[z, d],
+                    (self.dp, 2 * self.deep + 1 - self.core),
+                )
+            return carry
+
+        lax.fori_loop(0, self.nz, go, 0)
+
+    def wait(self, sem, ref):
+        pltpu.make_async_copy(ref, ref, sem).wait()
+
+    def start_dp(self):
+        self.wait(self.recv[0], self.got_core)
+
+        def add(z, carry):
+            for d in range(self.nd):
+                own = self.source[pl.ds(self.rows_of(2 * z + self.core, d), self.unit.part), :]
+                self.sum_core[d, z] = (own.astype(F32) + self.got_core[z, d].astype(F32)).astype(BF16)
+            return carry
+
+        lax.fori_loop(0, self.nz, add, 0)
+        for i in range(1, self.nd):
+            other = lax.rem(self.dp + i, self.nd)
+            self.push(1, self.sum_core.at[other], self.got_dp.at[i - 1], (other, self.fs))
+
+    def start_rest(self):
+        self.wait(self.recv[1], self.got_dp)
+
+        def add(z, carry):
+            total = self.sum_core[self.dp, z].astype(F32)
+            for i in range(self.nd - 1):
+                total = total + self.got_dp[i, z].astype(F32)
+            self.sum_dp[z] = total.astype(BF16)
+            return carry
+
+        lax.fori_loop(0, self.nz, add, 0)
+        for i in range(1, self.nz):
+            other = lax.rem(self.deep + i, self.nz)
+            self.push(2, self.sum_dp.at[other], self.got_rest.at[i - 1], (self.dp, 2 * other + self.core))
+
+    def start_copies(self):
+        self.wait(self.recv[2], self.got_rest)
+        total = self.sum_dp[self.deep].astype(F32)
+        for i in range(self.nz - 1):
+            total = total + self.got_rest[i].astype(F32)
+        rows = pl.ds(pl.multiple_of(self.dp * self.unit.part, 16), self.unit.part)
+        self.result[rows, :] = total.astype(BF16)
+        for i in range(1, self.nd):
+            other = lax.rem(self.dp + i, self.nd)
+            self.push(3, self.result.at[rows], self.result.at[rows], (other, self.fs))
+
+    def complete(self):
+        others = self.result.at[pl.ds(0, (self.nd - 1) * self.unit.part)]
+        self.wait(self.recv[3], others)
+        self.wait(self.send[0], self.got_core)
+        self.wait(self.send[1], self.got_dp)
+        self.wait(self.send[2], self.got_rest)
+        self.wait(self.send[3], others)
+
+
+def reduce_kernel(unit, source, result, *refs):
+    enter(unit.plan)
+    work = Reduction(unit, source, result, refs)
+    entered(unit.plan)
+    work.start_core()
+    work.start_dp()
+    work.start_rest()
+    work.start_copies()
+    work.complete()
+
+
+def reduce_last(plan, packed):
+    unit = plan.layer_unit()
+    return pl.pallas_call(
+        functools.partial(reduce_kernel, unit),
+        out_shape=jax.ShapeDtypeStruct((unit.owned, unit.width), BF16),
+        in_specs=[VM],
+        out_specs=VM,
+        scratch_shapes=Reduction.scratch(unit),
+        compiler_params=pltpu.CompilerParams(
+            collective_id=5, has_side_effects=True, vmem_limit_bytes=VMEM_LIMIT
+        ),
+        name="reduce_last",
+    )(packed)
 
 
 def taps():
@@ -529,11 +675,11 @@
 
         over_tiles(plan, start // LANE, width // LANE, chunk_back, back, 2, put_sums)
         share(plan, *ex_grad[g], sums[0:1, cols], sums[1:2, cols])
-    grad_head[:, C + LANE :] = dot(pool_low.T, grad_low).astype(BF16)
+    grad_head[0:hd, C + LANE :] = dot(pool_low.T, grad_low).astype(BF16)
     norm_grads = jnp.concatenate(
         [sums[1:2, :], sums[0:1, :], jnp.zeros((LANE - 2, hd), F32)], axis=0
     )
-    grad_head[:, C : C + LANE] = norm_grads.T.astype(BF16)
+    grad_head[0:hd, C : C + LANE] = norm_grads.T.astype(BF16)
     for g, (start, width) in enumerate(halves):
         cols = slice(start, start + width)
         shift_total, gain_total = collect(plan, *ex_grad[g])
@@ -573,7 +719,7 @@
         functools.partial(head_kernel, plan),
         out_shape=(
             jax.ShapeDtypeStruct((plan.rows, C), F32),
-            jax.ShapeDtypeStruct((hd, HEAD_W), BF16),
+            jax.ShapeDtypeStruct((plan.head_flat, HEAD_W), BF16),
             jax.ShapeDtypeStruct((2, KP), F32),
         ),
         in_specs=[VM] * 7,
@@ -605,10 +751,11 @@
     )
 
 
-def backward_kernel(plan, x, grad, expanded, depth, projected, stat_e, stat_c, pooled, presq, gate, we, wp, wr, wx, small, tail, *refs):
-    grad_x, packed = refs[:2]
-    turned, act, flow, low_proj, gated, sums, coef, squeeze_grad, flat = refs[2:11]
-    ex = exchange_refs(refs[11:], 2 * GROUPS + 1)
+def backward_kernel(plan, x, grad, expanded, depth, projected, stat_e, stat_c, pooled, presq, gate, we, wp, wr, wx, small, tail, later, *refs, unit):
+    grad_x, packed, summed = refs[:3]
+    turned, act, flow, low_proj, gated, sums, coef, squeeze_grad, flat, pair_buf = refs[3:13]
+    ex = exchange_refs(refs[13:], 2 * GROUPS + 1)
+    work = Reduction(unit, later, summed, refs[13 + 3 * (2 * GROUPS + 1) :])
     ex_two, ex_one, ex_three = ex[:GROUPS], ex[GROUPS : 2 * GROUPS], ex[2 * GROUPS]
     n = plan.images
     lane = lax.broadcasted_iota(jnp.int32, (1, LANE), 1)
@@ -621,6 +768,7 @@
     )
     entered(plan)
     share(plan, *ex_three, s, q)
+    work.start_core()
     bias_three, gain_three = s, q
 
     def chunk_two(j):
@@ -659,6 +807,7 @@
         return carry
 
     lax.fori_loop(0, PIX // MBLK, into_gated, 0)
+    work.start_dp()
 
     def gate_back(j, b, hoisted, totals):
         total = None
@@ -718,6 +867,7 @@
         over_tiles(plan, g * (GW // LANE), GW // LANE, chunk_norm, back_two, 2, put_sums(11))
         share(plan, *ex_two[g], sums[12:13, cols], sums[11:12, cols])
 
+    work.start_rest()
     proj_turned = low_proj[...].astype(F32).T.astype(BF16)
     for j in range(NJ):
         part = dot(proj_turned, gated[:, j * LANE : (j + 1) * LANE])
@@ -777,9 +927,9 @@
         over_tiles(plan, g * (GW // LANE), GW // LANE, chunk_one, back_one, 11, put_sums(0))
         share(plan, *ex_one[g], sums[10:11, cols], sums[9:10, cols])
 
+    work.start_copies()
     for j in range(NJ):
         flat[pl.ds(ROW_D + j, 14, stride=NJ), :] = sums[0:14, j * LANE : (j + 1) * LANE]
-    pair_buf = refs[11 + 3 * (2 * GROUPS + 1)]
     pair_buf[...] = grad_wr
     evens = pair_buf[pl.ds(0, E // 2, stride=2), :]
     odds = pair_buf[pl.ds(1, E // 2, stride=2), :]
@@ -817,25 +967,24 @@
             flat[pl.ds(j, C, stride=NJ), :] = dot(
                 turned[...], gated[:, j * LANE : (j + 1) * LANE]
             )
-    for f in range(plan.nf):
-        packed[f * plan.chunk : (f + 1) * plan.chunk, :] = flat[
-            plan.base[f] : plan.base[f] + plan.chunk, :
-        ].astype(BF16)
+    packed[...] = flat[...].astype(BF16)
+    work.complete()
     for e in ex:
         finish(plan, *e)
 
 
-def backward(plan, x, grad, kept, weights):
+def backward(plan, x, grad, kept, weights, later, unit, collective_id):
     n = plan.images
     big = (PIX, n, E)
     return pl.pallas_call(
-        functools.partial(backward_kernel, plan),
+        functools.partial(backward_kernel, plan, unit=unit),
         out_shape=(
             jax.ShapeDtypeStruct((plan.rows, C), F32),
-            jax.ShapeDtypeStruct((plan.nf * plan.chunk, LANE), BF16),
+            jax.ShapeDtypeStruct((plan.flat, LANE), BF16),
+            jax.ShapeDtypeStruct((unit.owned, unit.width), BF16),
         ),
-        in_specs=[VM] * 16,
-        out_specs=(VM,) * 2,
+        in_specs=[VM] * 17,
+        out_specs=(VM,) * 3,
         scratch_shapes=[
             pltpu.VMEM((C, plan.rows), BF16),
             pltpu.VMEM(big, F32),
@@ -846,14 +995,15 @@
             pltpu.VMEM((8, E), F32),
             pltpu.VMEM((n, E), F32),
             pltpu.VMEM((plan.flat, LANE), F32),
+            pltpu.VMEM((E, LANE), F32),
         ]
         + exchange_scratch(plan, [GW] * (2 * GROUPS) + [C])
-        + [pltpu.VMEM((E, LANE), F32)],
+        + Reduction.scratch(unit),
         compiler_params=pltpu.CompilerParams(
-            collective_id=3, has_side_effects=True, vmem_limit_bytes=VMEM_LIMIT
+            collective_id=collective_id, has_side_effects=True, vmem_limit_bytes=VMEM_LIMIT
         ),
         name="layer_backward",
-    )(x, grad, *kept, *weights)
+    )(x, grad, *kept, *weights, later)
 
 
 def adam_update(master, first, second, average, grad):
@@ -907,12 +1057,15 @@
     grad, head_grad, totals = head(plan, stream, w_head, bias, labels, partner, mix_weight)
     loss_sum = totals[1, 0]
     grad_bias = totals[0, :K]
-    head_grad = lax.psum_scatter(head_grad, "fsdp", scatter_dimension=0, tiled=True)
-    block_grads = [None] * LAYERS
+    later, unit, sums = head_grad, plan.head_unit(), []
     for layer in reversed(range(LAYERS)):
-        grad, packed = backward(plan, inputs[layer], grad, kept[layer], weights[layer])
-        block_grads[layer] = lax.psum_scatter(packed, "fsdp", scatter_dimension=0, tiled=True)
-    block_grad, head_grad = lax.psum((jnp.stack(block_grads), head_grad), "dp")
+        grad, later_next, summed = backward(
+            plan, inputs[layer], grad, kept[layer], weights[layer], later, unit, 3 + len(sums[:1])
+        )
+        sums.append(summed)
+        later, unit = later_next, plan.layer_unit()
+    sums.append(reduce_last(plan, later))
+    head_grad, block_grad = sums[0], jnp.stack(sums[:0:-1])
     block_grad = lax.dynamic_slice(
         block_grad.reshape(LAYERS, plan.chunk * LANE), (0, offset), (LAYERS, plan.shard)
     ).astype(F32)

time: 660 us -> 505 us (0.77)
  waiting for transfers between devices: 229 us -> 15.8 us
  Pallas kernels: 370 us -> 426 us
    reduce_scatter x4 -> x0, waiting for transfers between devices: 151 us -> none  [the longest x3 108 us: on_device(): lax.psum_scatter(packed, 'fsdp', scatter_dimension=0, tiled=True)]
    psum x1 -> x0, waiting for transfers between devices: 61.1 us -> none  [on_device(): block_grad, head_grad = lax.psum((jnp.stack(block_grads), head_grad), 'dp')]
    pallas_call x3 -> x4, Pallas kernels: 168 us -> 224 us  [the longest x3 191 us: backward(): pl.pallas_call(functools.partial(backward_kernel, plan, unit=unit), out_s...]
  transfers between devices with their start and end apart: 9 -> 4, of which waited for: 6 -> 1; matrix products, arithmetic and copies ran while one was open for 2% -> 2% of each run, Pallas kernels for 25% -> 33%
where the time goes in v2:
time: 505 us; the launch traced here: 497 us
  Pallas kernels  426 us (84%)
  local copies, waits for them, and re-layouts  25.5 us (5%)
  waiting for transfers between devices  15.8 us (3%)
  other arithmetic  14.7 us (3%)
  between operations  14.7 us (3%)
    pallas_call x3, Pallas kernels, backward(): pl.pallas_call(functools.partial(backward_kernel, plan, unit=unit), out_s...  191 us
    pallas_call x3, Pallas kernels, forward(): pl.pallas_call(functools.partial(forward_kernel, plan), out_shape=(jax.Sh...  149 us
    pallas_call x1, Pallas kernels, head(): pl.pallas_call(functools.partial(head_kernel, plan), out_shape=(jax.Shape...  37.3 us
    pallas_call x1, Pallas kernels, reduce_last(): pl.pallas_call(functools.partial(reduce_kernel, unit), out_shape=jax.Shap...  32.8 us
    all_gather x3, waiting for transfers between devices, on_device(): lax.all_gather(flat.reshape(plan.chunk, LANE), 'fsdp', axis=0, tiled=True)  15.7 us
    add x3, other arithmetic, adam_update(): average_new = EMA_RATE * average + (1.0 - EMA_RATE) * master_new  11.5 us
    pallas_call x3, Pallas kernels, unpack(): pl.pallas_call(functools.partial(unpack_kernel, plan), out_shape=(jax.Sha...  11 us
  transfers between devices with their start and end apart: 4, of which 1 were waited for; matrix products, arithmetic and copies ran while one was open for 2% of the time, Pallas kernels for 33%

profile of v2, /device:TPU:0, one launch (start us, length us, event | category | flops | bytes accessed | tf_op | source)
XLA Modules:
  0.0 497.4 jit_solution(18139799787283177564)
XLA Ops:
  7.2 1.9 convert.5
  9.2 4.2 slice_reduce_fusion
  13.4 2.4 dynamic_update_slice.9
  15.8 0.7 copy-done.8
  16.6 2.4 dynamic_update_slice.10
  19.7 2.4 dynamic_update_slice.11
  23.0 0.8 reshape.77
  24.0 0.9 concatenate.7
  25.0 0.7 copy.29.partner
  25.7 0.7 copy.30.weight
  26.4 0.7 copy.31.label
  27.7 5.1 %mix.1.x = f32[1024,256]{1,0:T(8,128)} custom-call(bf16[1024,256]{1,0:T(8,128)(2,1)} %bitcast.29, s32[64,1]{1,0:T(8,128)} %copy.29.partner, f32[64,1]{1,0:T(8,128)} %copy.30.weight), custom_call_target="tpu_custom_call" | custom-call | tf_op jit(solution)/shard_map/mix/pallas_call | solution.py:412
  32.8 15.7 %all-gather.5.cloned.1.call-done.got = bf16[8192,128]{1,0:T(8,128)(2,1)} async-done(((bf16[1024,128]{1,0:T(8,128)(2,1)}), bf16[8192,128]{1,0:T(8,128)(2,1)}) %all-gather.5.cloned.1.call-update) | async-done | bytes 2097168 | tf_op jit(solution)/shard_map/all_gather | solution.py:1034
  48.4 3.6 unpack.3
  52.1 57.0 %layer_forward.3 = (f32[1024,256]{1,0:T(8,128)}, f32[16,64,1536]{2,1,0:T(8,128)}, f32[16,64,1536]{2,1,0:T(8,128)}, f32[1024,256]{1,0:T(8,128)}, f32[8,1536]{1,0:...) custom-call(f32[1024,256]{1,0:T(8,128)} %mix.1.x, ...), custom_call_target="tpu_custom_call" | custom-call | tf_op jit(solution)/shard_map/layer_forward/pallas_call | solution.py:548
  109.1 3.7 unpack.4
  112.8 46.2 %layer_forward.4 = (f32[1024,256]{1,0:T(8,128)}, f32[16,64,1536]{2,1,0:T(8,128)}, f32[16,64,1536]{2,1,0:T(8,128)}, f32[1024,256]{1,0:T(8,128)}, f32[8,1536]{1,0:...) custom-call(f32[1024,256]{1,0:T(8,128)} %get-tuple-element.75.x, ...), custom_call_target="tpu_custom_call" | custom-call | tf_op jit(solution)/shard_map/layer_forward/pallas_call | solution.py:548
  159.0 3.6 unpack.5
  162.7 46.2 %layer_forward.5 = (f32[1024,256]{1,0:T(8,128)}, f32[16,64,1536]{2,1,0:T(8,128)}, f32[16,64,1536]{2,1,0:T(8,128)}, f32[1024,256]{1,0:T(8,128)}, f32[8,1536]{1,0:...) custom-call(f32[1024,256]{1,0:T(8,128)} %get-tuple-element.82.x, ...), custom_call_target="tpu_custom_call" | custom-call | tf_op jit(solution)/shard_map/layer_forward/pallas_call | solution.py:548
  208.9 37.3 %head.1 = (f32[1024,256]{1,0:T(8,128)}, bf16[1312,1408]{1,0:T(8,128)(2,1)}, f32[2,1024]{1,0:T(2,128)}) custom-call(f32[1024,256]{1,0:T(8,128)} %get-tuple-element.89.x, bf16[1280,1408]{1,0:T(8,128)(2,1)} %all-gather.11.cloned.1.call-done.w_head, f32[1,1024]{1,0:T(1,128)} %bitcast.33, s32[64,1]{1,0:T(8,128)} %copy.31.label, s32[1,64]{1,0:T(1,128)} %bitcast.34, ...), custom_call_target="tpu_custom_call" | custom-call | tf_op jit(solution)/shard_map/head/pallas_call | solution.py:718
  246.2 1.2 slice.38
  247.4 0.7 slice.42
  248.1 75.0 %layer_backward.3 = (f32[1024,256]{1,0:T(8,128)}, bf16[7888,128]{1,0:T(8,128)(2,1)}, bf16[192,1408]{1,0:T(8,128)(2,1)}) custom-call(f32[1024,256]{1,0:T(8,128)} %get-tuple-element.82.x, f32[1024,256]{1,0:T(8,128)} %get-tuple-element.91.grad, f32[16,64,1536]{2,1,0:T(8,128)} %get-tuple-element.92.expanded, f32[16,64,1536]{2,1,0:T(8,128)} %get-tuple-element.93.depth, ...), custom_call_target="tpu_custom_call" | custom-call | tf_op jit(solution)/shard_map/layer_backward/pallas_call | solution.py:979
  323.1 1.1 slice_convert_fusion
  324.2 57.7 %layer_backward.4 = (f32[1024,256]{1,0:T(8,128)}, bf16[7888,128]{1,0:T(8,128)(2,1)}, bf16[1024,128]{1,0:T(8,128)(2,1)}) custom-call(f32[1024,256]{1,0:T(8,128)} %get-tuple-element.75.x, f32[1024,256]{1,0:T(8,128)} %get-tuple-element.101.grad, f32[16,64,1536]{2,1,0:T(8,128)} %get-tuple-element.102.expanded, f32[16,64,1536]{2,1,0:T(8,128)} %get-tuple-element.103.depth, ...), custom_call_target="tpu_custom_call" | custom-call | tf_op jit(solution)/shard_map/layer_backward/pallas_call | solution.py:979
  382.0 58.2 %layer_backward.5 = (f32[1024,256]{1,0:T(8,128)}, bf16[7888,128]{1,0:T(8,128)(2,1)}, bf16[1024,128]{1,0:T(8,128)(2,1)}) custom-call(f32[1024,256]{1,0:T(8,128)} %mix.1.x, f32[1024,256]{1,0:T(8,128)} %get-tuple-element.111.grad, f32[16,64,1536]{2,1,0:T(8,128)} %get-tuple-element.112.expanded, f32[16,64,1536]{2,1,0:T(8,128)} %get-tuple-element.113.depth, ...), custom_call_target="tpu_custom_call" | custom-call | tf_op jit(solution)/shard_map/layer_backward/pallas_call | solution.py:979
  440.2 32.8 %reduce_last.1 = bf16[1024,128]{1,0:T(8,128)(2,1)} custom-call(bf16[7888,128]{1,0:T(8,128)(2,1)} %get-tuple-element.121.source), custom_call_target="tpu_custom_call" | custom-call | tf_op jit(solution)/shard_map/reduce_last/pallas_call | solution.py:279
  473.0 2.1 copy.40
  476.0 2.0 copy_bitcast_fusion
  478.7 3.7 add_multiply_fusion.1
  482.3 0.9 copy-done.6
  483.2 7.2 %add_multiply_fusion = (f32[3,125640]{1,0:T(4,128)}, f32[3,125640]{1,0:T(4,128)}, f32[3,125640]{1,0:T(4,128)}, f32[3,125640]{1,0:T(4,128)}) fusion(f32[3,125640]{1,0:T(4,128)S(1)} %copy-done.5, f32[3,125640]{1,0:T(4,128)S(1)} %copy-done, f32[3,125640]{1,0:T(4,128)S(1)} %copy-done.6, f32[3,125640]{1,0:T(4,128)S(1)} %copy-done.7, s32[]{:T(128)S(6)} %select_n.12, ...), kind=kLoop, calls=%fused_computation.3 | loop fusion | flops 7538400 | bytes 12847876 | tf_op jit(solution)/shard_map/add | solution.py:1017
  (63 shorter events, 4.0 us)
Async XLA Ops:
  7.2 41.3 %all-gather.5.cloned.1.call-start = ((), (), s32[]{:S(2)}) async-start(), calls=%async_computation | async-start | bytes 2359296 | tf_op jit(solution)/shard_map/all_gather | solution.py:1034
  13.3 9.6 %copy-start.2 = (f32[201280]{0:T(1024)S(1)}, f32[201280]{0:T(1024)}, u32[]{:S(2)}) copy-start(f32[201280]{0:T(1024)} %param.24) | copy-start | bytes 2415364
  15.7 0.7 copy-start.8
  16.5 92.6 %all-gather.7.cloned.1.call-start = ((), (), s32[]{:S(2)}) async-start(), calls=%async_computation.1 | async-start | bytes 2359296 | tf_op jit(solution)/shard_map/all_gather | solution.py:1034
  18.9 0.7 copy-start.9
  19.7 139.4 %all-gather.9.cloned.1.call-start = ((), (), s32[]{:S(2)}) async-start(), calls=%async_computation.2 | async-start | bytes 2359296 | tf_op jit(solution)/shard_map/all_gather | solution.py:1034
  22.1 0.7 copy-start.10
  22.8 2.1 copy-start.17
  22.9 2.8 copy-start.18
  22.9 3.5 copy-start.16
  22.9 4.2 copy-start.12
  22.9 186.0 %all-gather.11.cloned.1.call-start = ((), (), s32[]{:S(2)}) async-start(), calls=%async_computation.3 | async-start | bytes 4055040 | tf_op jit(solution)/shard_map/all_gather | solution.py:1047
  324.2 57.8 %copy-start.1 = (f32[160,1408]{1,0:T(8,128)}, f32[160,1408]{1,0:T(8,128)S(1)}, u32[]{:S(2)}) copy-start(f32[160,1408]{1,0:T(8,128)S(1)} %slice_convert_fusion) | copy-start | bytes 2703364
  440.2 35.0 %slice-start = ((f32[160,1408]{1,0:T(8,128)}), f32[160,258]{1,0:T(8,128)S(1)}, s32[]{:S(2)}) async-start(f32[160,1408]{1,0:T(8,128)} %copy-done.1), calls=%async_computation.4 | async-start | bytes 491520 | tf_op jit(solution)/shard_map/slice | solution.py:1074
  440.2 35.0 %slice-start.1 = ((f32[160,1408]{1,0:T(8,128)}), f32[160,1000]{1,0:T(8,128)S(1)}, s32[]{:S(2)}) async-start(f32[160,1408]{1,0:T(8,128)} %copy-done.1), calls=%async_computation.5 | async-start | bytes 1310720 | tf_op jit(solution)/shard_map/slice | solution.py:1074
  475.4 2.5 copy-start.13
  475.4 2.5 copy-start.14
  475.4 2.5 copy-start.15
  475.5 3.2 copy-start.3
  475.5 3.1 copy-start.11
  476.0 6.4 %copy-start.7 = (f32[3,125640]{1,0:T(4,128)S(1)}, f32[3,125640]{1,0:T(4,128)}, u32[]{:S(2)}) copy-start(f32[3,125640]{1,0:T(4,128)} %param.22) | copy-start | bytes 4523044
  478.6 3.7 copy-start
  478.6 3.7 copy-start.4
  478.6 3.7 copy-start.5
  478.6 4.6 copy-start.6
Sparse Core Ops, SparseCore 0:
  16.6 31.7 all-gather.4
  50.6 45.2 all-gather.6
  97.5 33.4 all-gather.8
  132.5 50.1 all-gather.10
